TPU v7x, 32 devices: a whole 2x2x4 slice. The times are simulated.
32 devices in a mesh: dp: 4 (over y, x), member: 2 (over core), expert: 4 (over z).
Axes of the slice: x: 2, y: 2, z: 4, core: 2. Of those that a mesh axis runs over, the one named last changes fastest.
Arguments:
- tokens: bfloat16 [1024, 1280], P(('dp', 'member')), may hold values from -6 to 6
- route_ids: int32 [2, 1024, 1], P(None, ('dp', 'member')), may hold values from 0 to 3; in each aligned block of 128 rows (0 to 127, 128 to 255, ..., all dimensions but the last counted through in order) at most 48 rows name the same one
- router: float32 [2, 1280, 4], replicated, may hold values from -0.15625 to 0.15625
- w_in: bfloat16 [2, 4, 1280, 4608], P('member', 'dp', None, 'expert'), may hold values from -0.15625 to 0.15625
- w_out: bfloat16 [2, 4, 4608, 1280], P('member', 'dp', 'expert'), may hold values from -0.09375 to 0.09375
- out_grad: bfloat16 [2, 1024, 1280], P(None, ('dp', 'member')), may hold values from -6 to 6
Outputs:
- moe_out: bfloat16 [2, 1024, 1280], P(None, ('dp', 'member'))
- token_grad: float32 [1024, 1280], P(('dp', 'member'))
- first_grad: bfloat16 [2, 4, 1280, 4608], P('member', 'dp', None, 'expert')
- second_grad: bfloat16 [2, 4, 4608, 1280], P('member', 'dp', 'expert')
- router_grad: float32 [2, 1280, 4], replicated
Inputs may be any that keep to these rules, and one draw needn't show every extreme that they name: `route_ids`: in each aligned block of 128 rows of one member no expert is named by more than 48 rows, and some block names some expert exactly 48 times.
All inputs are finite; a program needn't handle non-finite values.
Results may differ from a plain program's by a relative error of at most 0.022.
Values may be sent and summed in bfloat16 or wider, within the bound.
A program may use at most 64 MiB of HBM per device.

v0:
```python
import jax
import jax.numpy as jnp
from jax import lax
from jax.sharding import PartitionSpec as P

tanh_scale = 0.7978845608028654
cubic_term = 0.044715


def gelu_pair(pre_act):
    inner = tanh_scale * (pre_act + cubic_term * pre_act * pre_act * pre_act)
    tanh_value = jnp.tanh(inner)
    value = 0.5 * pre_act * (1.0 + tanh_value)
    gelu_slope = 0.5 * (1.0 + tanh_value) + 0.5 * pre_act * (
        1.0 - tanh_value * tanh_value
    ) * tanh_scale * (1.0 + 3.0 * cubic_term * pre_act * pre_act)
    return (value, gelu_slope)


def slot_rank(expert_ids, experts):
    hot_table = (expert_ids[..., None] == jnp.arange(experts, dtype=jnp.int32)).astype(jnp.int32)
    earlier = jnp.cumsum(hot_table, axis=-2) - hot_table
    return jnp.sum(earlier * hot_table, axis=-1)


def dispatch(x_send, g_send, experts, members, capacity):
    row_width = x_send.shape[1]
    arrived = (
        lax.all_to_all(
            x_send.reshape(experts * members, capacity, row_width),
            ("dp", "member"),
            split_axis=0,
            concat_axis=0,
            tiled=True,
        ),
        lax.all_to_all(
            g_send.reshape(experts * members, capacity, row_width),
            ("dp", "member"),
            split_axis=0,
            concat_axis=0,
            tiled=True,
        ),
    )
    return (arrived[0].reshape(-1, row_width), arrived[1].reshape(-1, row_width))


def send_back(first_rows, second_rows, capacity):
    row_width = first_rows.shape[1]
    dp_count = lax.axis_size("dp")
    member_count = lax.axis_size("member")
    arrived = (
        lax.all_to_all(
            first_rows.reshape(dp_count * member_count, capacity, row_width),
            ("dp", "member"),
            split_axis=0,
            concat_axis=0,
            tiled=True,
        ),
        lax.all_to_all(
            second_rows.reshape(dp_count * member_count, capacity, row_width),
            ("dp", "member"),
            split_axis=0,
            concat_axis=0,
            tiled=True,
        ),
    )
    return (arrived[0].reshape(-1, row_width), arrived[1].reshape(-1, row_width))


def block_sums(first_part, second_part):
    return (
        lax.psum(first_part, "expert").astype(jnp.float32),
        lax.psum(second_part, "expert").astype(jnp.float32),
    )


def shards(tokens, route_ids, router, w_in, w_out, out_grad):
    members = route_ids.shape[0]
    tok_rows = route_ids.shape[1]
    experts = router.shape[2]
    model_width = tokens.shape[1]
    capacity = max(2, 3 * tok_rows // (2 * experts))
    expert_ids = route_ids[:, :, 0]
    slot_rows = slot_rank(expert_ids, experts)
    member_index = jnp.arange(members, dtype=jnp.int32)[:, None]
    buffer_index = ((expert_ids * members + member_index) * capacity + slot_rows).reshape(-1)
    tokens_f = tokens.astype(jnp.float32)
    hot_table = (expert_ids[..., None] == jnp.arange(experts, dtype=jnp.int32)).astype(jnp.float32)
    logits = jnp.einsum("td,mde->mte", tokens_f, router, precision=lax.Precision.HIGHEST)
    gate_value = jax.nn.sigmoid(jnp.sum(logits * hot_table, axis=-1))
    scaled = (gate_value[..., None] * out_grad.astype(jnp.float32)).astype(jnp.bfloat16)
    total_rows = experts * members * capacity
    token_copies = jnp.broadcast_to(tokens[None], (members, tok_rows, model_width)).reshape(
        -1, model_width
    )
    x_send = jnp.zeros((total_rows, model_width), jnp.bfloat16).at[buffer_index].set(token_copies)
    g_send = (
        jnp.zeros((total_rows, model_width), jnp.bfloat16)
        .at[buffer_index]
        .set(scaled.reshape(-1, model_width))
    )
    x_rows, g_rows = dispatch(x_send, g_send, experts, members, capacity)
    w_first = w_in[0, 0]
    w_second = w_out[0, 0]
    pre_act = jnp.dot(x_rows, w_first, preferred_element_type=jnp.float32)
    act_value, gelu_slope = gelu_pair(pre_act)
    activation = act_value.astype(jnp.bfloat16)
    hidden_grad = jnp.einsum("rd,hd->rh", g_rows, w_second, preferred_element_type=jnp.float32)
    pre_grad = (hidden_grad * gelu_slope).astype(jnp.bfloat16)
    grad_first = jnp.einsum("rd,rh->dh", x_rows, pre_grad, preferred_element_type=jnp.float32)
    grad_second = jnp.einsum("rh,rd->hd", activation, g_rows, preferred_element_type=jnp.float32)
    part_out = jnp.dot(activation, w_second, preferred_element_type=jnp.float32).astype(
        jnp.bfloat16
    )
    part_dx = jnp.einsum("rh,dh->rd", pre_grad, w_first, preferred_element_type=jnp.float32).astype(
        jnp.bfloat16
    )
    out_total, dx_total = block_sums(part_out, part_dx)
    back_out, back_dx = send_back(
        out_total.astype(jnp.bfloat16), dx_total.astype(jnp.bfloat16), capacity
    )
    expert_output = back_out[buffer_index].reshape(members, tok_rows, model_width)
    expert_dx = back_dx[buffer_index].reshape(members, tok_rows, model_width)
    output_f = expert_output.astype(jnp.float32)
    moe_out = (gate_value[..., None] * output_f).astype(jnp.bfloat16)
    gate_grad = jnp.sum(out_grad.astype(jnp.float32) * output_f, axis=-1)
    logit_grad = gate_grad * gate_value * (1.0 - gate_value)
    weighted = hot_table * logit_grad[..., None]
    router_local = jnp.einsum("td,mte->mde", tokens_f, weighted, precision=lax.Precision.HIGHEST)
    router_grad = lax.psum(router_local, ("dp", "member"))
    router_term = jnp.einsum("mte,mde->td", weighted, router, precision=lax.Precision.HIGHEST)
    token_grad = router_term + jnp.sum(expert_dx.astype(jnp.float32), axis=0)
    first_grad = grad_first.astype(jnp.bfloat16)[None, None]
    second_grad = grad_second.astype(jnp.bfloat16)[None, None]
    return (moe_out, token_grad, first_grad, second_grad, router_grad)


def solution(mesh):
    in_specs = (
        P(("dp", "member"), None),
        P(None, ("dp", "member"), None),
        P(),
        P("member", "dp", None, "expert"),
        P("member", "dp", "expert", None),
        P(None, ("dp", "member"), None),
    )
    out_specs = (
        P(None, ("dp", "member"), None),
        P(("dp", "member"), None),
        P("member", "dp", None, "expert"),
        P("member", "dp", "expert", None),
        P(),
    )
    return jax.shard_map(shards, mesh=mesh, in_specs=in_specs, out_specs=out_specs, check_vma=False)
```

profile of v0, /device:TPU:0, one launch (start us, length us, event | category | flops | bytes accessed | tf_op | source)
XLA Modules:
  0.0 217.5 jit_solution(8025667506543282775)
XLA Ops:
  7.2 0.0 copy-start
  7.2 0.8 fusion.37
  8.0 0.1 copy.11
  8.2 0.2 reduce_window_sum.11
  8.4 0.1 copy.12
  8.4 0.7 select_reduce_fusion
  9.1 0.7 compare_select_fusion
  9.8 0.0 copy-start.3
  9.9 1.9 broadcast_in_dim.6
  11.8 3.3 %scatter_custom_fusion = bf16[384,1280]{1,0:T(8,128)(2,1)} fusion(s32[256]{0:T(256)S(1)} %bitcast.87, bf16[256,1280]{1,0:T(8,128)(2,1)} %bitcast.81, bf16[]{:T(256)} %constant.13.clone.1), kind=kCustom, calls=%fused_computation.42 | custom fusion | bytes 983552 | tf_op jit(solution)/shard_map/scatter | solution.py:96
  15.0 5.2 %all-to-all-start = ((bf16[8,48,1280]{2,1,0:T(8,128)(2,1)}), bf16[8,48,1280]{2,1,0:T(8,128)(2,1)}, u32[]{:S(2)}, u32[]{:S(2)}) async-start(bf16[8,48,1280]{2,1,0:T(8,128)(2,1)} %bitcast.76), calls=%async_computation | async-start | bytes 1966080 | tf_op jit(solution)/shard_map/all_to_all | solution.py:29
  20.2 0.0 copy-done.1
  20.2 0.0 copy-done.2
  20.2 0.0 copy-done.3
  20.2 0.4 fusion.28
  20.6 2.1 fusion.24
  22.7 3.3 %scatter_custom_fusion.1 = bf16[384,1280]{1,0:T(8,128)(2,1)} fusion(s32[256]{0:T(256)S(1)} %bitcast.88, bf16[256,1280]{1,0:T(8,128)(2,1)} %bitcast.80, bf16[]{:T(256)} %constant.13.clone.1), kind=kCustom, calls=%fused_computation.40 | custom fusion | bytes 983552 | tf_op jit(solution)/shard_map/scatter | solution.py:100
  26.0 9.0 %all-to-all-done = bf16[8,48,1280]{2,1,0:T(8,128)(2,1)} async-done(((bf16[8,48,1280]{2,1,0:T(8,128)(2,1)}), bf16[8,48,1280]{2,1,0:T(8,128)(2,1)}, u32[]{:S(2)}, u32[]{:S(2)}) %all-to-all-start) | async-done | bytes 983072 | tf_op jit(solution)/shard_map/all_to_all | solution.py:29
  35.0 4.2 %all-to-all-start.2 = ((bf16[8,48,1280]{2,1,0:T(8,128)(2,1)}), bf16[8,48,1280]{2,1,0:T(8,128)(2,1)}, u32[]{:S(2)}, u32[]{:S(2)}) async-start(bf16[8,48,1280]{2,1,0:T(8,128)(2,1)} %bitcast.75), calls=%async_computation.2 | async-start | bytes 1966080 | tf_op jit(solution)/shard_map/all_to_all | solution.py:36
  39.2 0.0 all-reduce.3.cloned.1.call-start
  39.3 3.6 %fusion.7 = f32[384,1152]{1,0:T(8,128)S(1)} fusion(bf16[384,1280]{1,0:T(8,128)(2,1)} %bitcast.9, bf16[1,1,1280,1152]{3,2,1,0:T(8,128)(2,1)} %param.9), kind=kOutput, calls=%fused_computation.14 | convolution fusion | flops 1132462080 | bytes 5701632 | tf_op jit(solution)/shard_map/dot_general | solution.py:105
  42.9 0.0 copy-start.5
  42.9 1.2 copy-done.5
  44.1 0.0 copy-done
  44.1 2.7 %fusion.15 = bf16[384,1280]{1,0:T(8,128)(2,1)} fusion(bf16[1,1,1152,1280]{3,2,1,0:T(8,128)(2,1)S(1)} %copy-done, f32[384,1152]{1,0:T(8,128)S(1)} %fusion.7), kind=kOutput, calls=%fused_computation.18 | convolution fusion | flops 1136934912 | bytes 5701632 | tf_op jit(solution)/shard_map/dot_general | solution.py:112
  46.8 7.2 %all-to-all-done.2 = bf16[8,48,1280]{2,1,0:T(8,128)(2,1)} async-done(((bf16[8,48,1280]{2,1,0:T(8,128)(2,1)}), bf16[8,48,1280]{2,1,0:T(8,128)(2,1)}, u32[]{:S(2)}, u32[]{:S(2)}) %all-to-all-start.2) | async-done | bytes 983072 | tf_op jit(solution)/shard_map/all_to_all | solution.py:36
  54.0 3.7 %fusion.9 = bf16[384,1152]{1,0:T(8,128)(2,1)S(1)} fusion(bf16[384,1280]{1,0:T(8,128)(2,1)} %bitcast.19, bf16[1,1,1152,1280]{3,2,1,0:T(8,128)(2,1)S(1)} %copy-done, f32[384,1152]{1,0:T(8,128)} %copy-done.5), kind=kOutput, calls=%fused_computation.16 | convolution fusion | flops 1140867072 | bytes 6586368 | tf_op jit(solution)/shard_map/rd,hd->rh/dot_general | solution.py:108
  57.7 0.0 copy-done.4
  57.7 0.0 copy-start.7
  57.7 2.4 %fusion.12 = bf16[384,1280]{1,0:T(8,128)(2,1)} fusion(bf16[384,1152]{1,0:T(8,128)(2,1)S(1)} %fusion.9, bf16[1,1,1280,1152]{3,2,1,0:T(8,128)(2,1)S(1)} %copy-done.4), kind=kOutput, calls=%fused_computation.17 | convolution fusion | flops 1132953600 | bytes 4816896 | tf_op jit(solution)/shard_map/rh,dh->rd/dot_general | solution.py:115
  60.2 0.0 copy-done.7
  60.2 0.0 all-reduce.3.cloned.1.call-update
  60.2 82.2 %all-reduce.3.cloned.1.call-done = (bf16[8,48,1280]{2,1,0:T(8,128)(2,1)}, bf16[8,48,1280]{2,1,0:T(8,128)(2,1)}) async-done(((bf16[8,48,1280]{2,1,0:T(8,128)(2,1)}, bf16[8,48,1280]{2,1,0:T(8,128)(2,1)}), (bf16[8,48,1280]{2,1,0:T(8,128)(2,1)}, bf16[8,48,1280]{2,1,0:T(8,128)(2,1)})) %all-reduce.3.cloned.1.call-update) | async-done | bytes 1966096 | tf_op jit(solution)/shard_map/psum | solution.py:72
  142.4 4.4 %all-to-all-start.1 = ((bf16[8,48,1280]{2,1,0:T(8,128)(2,1)}), bf16[8,48,1280]{2,1,0:T(8,128)(2,1)}, u32[]{:S(2)}, u32[]{:S(2)}) async-start(bf16[8,48,1280]{2,1,0:T(8,128)(2,1)} %get-tuple-element.5), calls=%async_computation.1 | async-start | bytes 1966080 | tf_op jit(solution)/shard_map/all_to_all | solution.py:52
  146.8 0.0 copy-start.6
  146.9 5.0 %fusion = bf16[1,1,1280,1152]{3,2,1,0:T(8,128)(2,1)} fusion(bf16[384,1280]{1,0:T(8,128)(2,1)} %bitcast.9, bf16[384,1152]{1,0:T(8,128)(2,1)} %copy-done.7), kind=kOutput, calls=%fused_computation.6 | convolution fusion | flops 1133936640 | bytes 4816896 | tf_op jit(solution)/shard_map/rd,rh->dh/dot_general | solution.py:110
  151.9 4.7 %fusion.1 = bf16[1,1,1152,1280]{3,2,1,0:T(8,128)(2,1)} fusion(bf16[384,1280]{1,0:T(8,128)(2,1)} %bitcast.19, f32[384,1152]{1,0:T(8,128)S(1)} %copy-done.6), kind=kOutput, calls=%fused_computation.7 | convolution fusion | flops 1137917952 | bytes 5701632 | tf_op jit(solution)/shard_map/rh,rd->hd/dot_general | solution.py:111
  156.6 4.8 %all-to-all-done.1 = bf16[8,48,1280]{2,1,0:T(8,128)(2,1)} async-done(((bf16[8,48,1280]{2,1,0:T(8,128)(2,1)}), bf16[8,48,1280]{2,1,0:T(8,128)(2,1)}, u32[]{:S(2)}, u32[]{:S(2)}) %all-to-all-start.1) | async-done | bytes 983072 | tf_op jit(solution)/shard_map/all_to_all | solution.py:52
  161.4 4.2 %all-to-all-start.3 = ((bf16[8,48,1280]{2,1,0:T(8,128)(2,1)}), bf16[8,48,1280]{2,1,0:T(8,128)(2,1)}, u32[]{:S(2)}, u32[]{:S(2)}) async-start(bf16[8,48,1280]{2,1,0:T(8,128)(2,1)} %get-tuple-element.6), calls=%async_computation.3 | async-start | bytes 1966080 | tf_op jit(solution)/shard_map/all_to_all | solution.py:59
  165.6 3.9 %gather_fusion = bf16[256,1280]{1,0:T(8,128)(2,1)} fusion(bf16[384,1280]{1,0:T(8,128)(2,1)} %bitcast.13, s32[1024]{0:T(1024)S(1)} %pad_clamp_fusion), kind=kCustom, calls=%fused_computation | custom fusion | bytes 1311744 | tf_op jit(solution)/shard_map/gather | solution.py:122
  169.6 1.5 fusion.26
  171.1 2.1 fusion.25
  173.2 7.1 %all-to-all-done.3 = bf16[8,48,1280]{2,1,0:T(8,128)(2,1)} async-done(((bf16[8,48,1280]{2,1,0:T(8,128)(2,1)}), bf16[8,48,1280]{2,1,0:T(8,128)(2,1)}, u32[]{:S(2)}, u32[]{:S(2)}) %all-to-all-start.3) | async-done | bytes 983072 | tf_op jit(solution)/shard_map/all_to_all | solution.py:59
  180.3 3.9 %gather_fusion.1 = bf16[256,1280]{1,0:T(8,128)(2,1)} fusion(bf16[384,1280]{1,0:T(8,128)(2,1)} %bitcast.21, s32[1024]{0:T(1024)S(1)} %pad_clamp_fusion), kind=kCustom, calls=%fused_computation.1 | custom fusion | bytes 1311744 | tf_op jit(solution)/shard_map/gather | solution.py:123
  184.3 1.2 convert_reduce_fusion
  185.5 0.2 convolution_bitcast_fusion.1
  185.8 1.6 fusion.18
  187.4 23.3 %psum.23 = f32[2,1280,4]{1,2,0:T(4,128)} all-reduce(f32[2,1280,4]{1,2,0:T(4,128)S(1)} %convolution_bitcast_fusion.1), channel_id=1, replica_groups=mesh['dp'=4,'member'=2,'expert'=4] {'dp','member'}, use_global_device_ids=true, to_apply=%region_9.10 | all-reduce | flops 10240 | bytes 81920 | tf_op jit(solution)/shard_map/psum | solution.py:130
  (8 shorter events, 0.0 us)
Async XLA Ops:
  7.2 36.9 %copy-start = (bf16[1,1,1152,1280]{3,2,1,0:T(8,128)(2,1)S(1)}, bf16[1,1,1152,1280]{3,2,1,0:T(8,128)(2,1)}, u32[]{:S(2)}) copy-start(bf16[1,1,1152,1280]{3,2,1,0:T(8,128)(2,1)} %param.10) | copy-start | bytes 8847364
  9.8 10.4 %copy-start.1 = (bf16[128,1280]{1,0:T(8,128)(2,1)S(1)}, bf16[128,1280]{1,0:T(8,128)(2,1)}, u32[]{:S(2)}) copy-start(bf16[128,1280]{1,0:T(8,128)(2,1)} %param.6) | copy-start | bytes 983044
  9.8 10.4 %copy-start.2 = (f32[2,1280,4]{1,2,0:T(4,128)S(1)}, f32[2,1280,4]{1,2,0:T(4,128)}, u32[]{:S(2)}) copy-start(f32[2,1280,4]{1,2,0:T(4,128)} %param.8) | copy-start | bytes 122884
  9.8 10.4 %copy-start.3 = (s32[2,128,1]{1,2,0:T(1,128)S(1)}, s32[2,128,1]{1,2,0:T(1,128)}, u32[]{:S(2)}) copy-start(s32[2,128,1]{1,2,0:T(1,128)} %param.7) | copy-start | bytes 3076
  15.0 20.0 %all-to-all-start = ((bf16[8,48,1280]{2,1,0:T(8,128)(2,1)}), bf16[8,48,1280]{2,1,0:T(8,128)(2,1)}, u32[]{:S(2)}, u32[]{:S(2)}) async-start(bf16[8,48,1280]{2,1,0:T(8,128)(2,1)} %bitcast.76), calls=%async_computation | async-start | bytes 1966080 | tf_op jit(solution)/shard_map/all_to_all | solution.py:29
  35.0 19.0 %all-to-all-start.2 = ((bf16[8,48,1280]{2,1,0:T(8,128)(2,1)}), bf16[8,48,1280]{2,1,0:T(8,128)(2,1)}, u32[]{:S(2)}, u32[]{:S(2)}) async-start(bf16[8,48,1280]{2,1,0:T(8,128)(2,1)} %bitcast.75), calls=%async_computation.2 | async-start | bytes 1966080 | tf_op jit(solution)/shard_map/all_to_all | solution.py:36
  39.2 103.2 %all-reduce.3.cloned.1.call-start = ((), (), s32[]{:S(2)}) async-start(), calls=%async_computation.4 | async-start | bytes 3932160 | tf_op jit(solution)/shard_map/psum | solution.py:72
  42.9 1.2 copy-start.5
  54.0 3.7 %copy-start.4 = (bf16[1,1,1280,1152]{3,2,1,0:T(8,128)(2,1)S(1)}, bf16[1,1,1280,1152]{3,2,1,0:T(8,128)(2,1)}, u32[]{:S(2)}) copy-start(bf16[1,1,1280,1152]{3,2,1,0:T(8,128)(2,1)} %param.9) | copy-start | bytes 8847364
  57.7 2.5 %copy-start.7 = (bf16[384,1152]{1,0:T(8,128)(2,1)}, bf16[384,1152]{1,0:T(8,128)(2,1)S(1)}, u32[]{:S(2)}) copy-start(bf16[384,1152]{1,0:T(8,128)(2,1)S(1)} %fusion.9) | copy-start | bytes 2654212
  142.4 18.9 %all-to-all-start.1 = ((bf16[8,48,1280]{2,1,0:T(8,128)(2,1)}), bf16[8,48,1280]{2,1,0:T(8,128)(2,1)}, u32[]{:S(2)}, u32[]{:S(2)}) async-start(bf16[8,48,1280]{2,1,0:T(8,128)(2,1)} %get-tuple-element.5), calls=%async_computation.1 | async-start | bytes 1966080 | tf_op jit(solution)/shard_map/all_to_all | solution.py:52
  146.8 5.0 %copy-start.6 = (f32[384,1152]{1,0:T(8,128)S(1)}, f32[384,1152]{1,0:T(8,128)}, u32[]{:S(2)}) copy-start(f32[384,1152]{1,0:T(8,128)} %copy-done.5) | copy-start | bytes 5308420
  161.4 19.0 %all-to-all-start.3 = ((bf16[8,48,1280]{2,1,0:T(8,128)(2,1)}), bf16[8,48,1280]{2,1,0:T(8,128)(2,1)}, u32[]{:S(2)}, u32[]{:S(2)}) async-start(bf16[8,48,1280]{2,1,0:T(8,128)(2,1)} %get-tuple-element.6), calls=%async_computation.3 | async-start | bytes 1966080 | tf_op jit(solution)/shard_map/all_to_all | solution.py:59
Sparse Core Ops, SparseCore 0:
  60.3 82.0 all-reduce.2
where the time goes:
time: 218 us
  waiting for transfers between devices  110 us (50%)
  matrix products  24.3 us (11%)
  blocking collectives  23.3 us (11%)
  starting transfers between devices  18.1 us (8%)
  local copies, waits for them, and re-layouts  17.8 us (8%)
  between operations  14.2 us (7%)
  other arithmetic  9.47 us (4%)
    psum x1, waiting for transfers between devices, block_sums(): lax.psum(first_part, 'expert').astype(jnp.float32)  82.2 us
    psum x1, blocking collectives, shards(): router_grad = lax.psum(router_local, ('dp', 'member'))  23.3 us
    all_to_all x1, waiting for transfers between devices, dispatch(): lax.all_to_all(x_send.reshape(experts * members, capacity, row_width), ('...  8.98 us
    all_to_all x1, waiting for transfers between devices, dispatch(): lax.all_to_all(g_send.reshape(experts * members, capacity, row_width), ('...  7.2 us
    all_to_all x1, waiting for transfers between devices, send_back(): lax.all_to_all(second_rows.reshape(dp_count * member_count, capacity, row...  7.12 us
    all_to_all x1, starting transfers between devices, dispatch(): lax.all_to_all(x_send.reshape(experts * members, capacity, row_width), ('...  5.17 us
    dot_general x1, matrix products, shards(): jnp.einsum('rd,rh->dh', x_rows, pre_grad, preferred_element_type=jnp.floa...  5.03 us
    all_to_all x1, waiting for transfers between devices, send_back(): lax.all_to_all(first_rows.reshape(dp_count * member_count, capacity, row_...  4.82 us
  transfers between devices with their start and end apart: 5, of which 5 were waited for; matrix products, arithmetic and copies ran while one was open for 13% of the time, Pallas kernels for 0%

commit v1 on v0

v1 whole, which is shorter than its diff:
```python
import functools

import jax
import jax.numpy as jnp
from jax import lax
from jax.experimental import pallas as pl
from jax.experimental.pallas import tpu as pltpu
from jax.sharding import PartitionSpec as P

MESH = pl.DeviceIdType.MESH
tanh_scale = 0.7978845608028654
cubic_term = 0.044715


def gelu_pair(pre_act):
    square = pre_act * pre_act
    tanh_value = jnp.tanh(tanh_scale * (pre_act + cubic_term * square * pre_act))
    half = 0.5 * (1.0 + tanh_value)
    slope = half + 0.5 * pre_act * (1.0 - tanh_value * tanh_value) * tanh_scale * (
        1.0 + 3.0 * cubic_term * square
    )
    return pre_act * half, slope


def slot_rank(expert_ids, experts):
    hot_table = (expert_ids[..., None] == jnp.arange(experts, dtype=jnp.int32)).astype(jnp.int32)
    earlier = jnp.cumsum(hot_table, axis=-2) - hot_table
    return jnp.sum(earlier * hot_table, axis=-1)


def dot(a, b, ca, cb, precision=None):
    return lax.dot_general(
        a, b, (((ca,), (cb,)), ((), ())), precision=precision, preferred_element_type=jnp.float32
    )


def tile_of(size, wanted):
    while size % wanted:
        wanted -= 128
    return wanted


def layer_kernel(
    cfg,
    x_send, g_send, w1_hbm, w2_hbm, unperm, tokens, out_grad, hot_rows, gate_slope,
    out_tot, dx_tot, first_hbm, second_hbm, router_all,
    w1, w2, xr, gr, act, slope, pg, po, pd, ro, rd, first, second,
    own, red, xch, res, router_part, router_z, router_sum,
    load_sem, x_ss, x_rs, g_ss, g_rs, o_ss, o_rs, d_ss, d_rs,
    red_ss, red_rs, xch_ss, xch_rs, res_ss, res_rs, rz_ss, rz_rs, rp_ss, rp_rs,
):
    dp, members, zn, cap, toks, chunk = cfg
    peers = dp * members
    me_dp, me_m, me_z = lax.axis_index("dp"), lax.axis_index("member"), lax.axis_index("expert")
    me = me_dp * members + me_m
    width = x_send.shape[-1]
    hidden = w1.shape[1]
    rows = peers * cap

    def plane(index):
        return {"dp": index // members, "member": index % members}

    def loop(count, body):
        lax.fori_loop(0, count, lambda i, c: (body(i), c)[1], 0)

    barrier = pltpu.get_barrier_semaphore()

    def greet_plane(i):
        pl.semaphore_signal(barrier, inc=1, device_id=plane((me + 1 + i) % peers), device_id_type=MESH)

    def greet_z(i):
        pl.semaphore_signal(
            barrier, inc=1, device_id={"expert": (me_z + 1 + i) % zn}, device_id_type=MESH
        )

    loop(peers - 1, greet_plane)
    loop(zn - 1, greet_z)
    load1 = pltpu.make_async_copy(w1_hbm, w1, load_sem.at[0])
    load2 = pltpu.make_async_copy(w2_hbm, w2, load_sem.at[1])
    load1.start()
    load2.start()
    pl.semaphore_wait(barrier, peers + zn - 2)

    def exchange(source, target, send_sem, recv_sem, slot, own_sem):
        def remote(peer):
            return pltpu.make_async_remote_copy(
                src_ref=source.at[peer],
                dst_ref=target.at[slot(me)],
                send_sem=send_sem.at[peer],
                recv_sem=recv_sem.at[me],
                device_id=plane(peer),
                device_id_type=MESH,
            )

        mine = pltpu.make_async_copy(source.at[me], target.at[slot(me)], own_sem)
        mine.start()
        loop(peers - 1, lambda i: remote((me + 1 + i) % peers).start())

        def wait_recv():
            mine.wait()

            def one(i):
                peer = (me + 1 + i) % peers
                pltpu.make_async_remote_copy(
                    src_ref=source.at[peer],
                    dst_ref=target.at[slot(peer)],
                    send_sem=send_sem.at[peer],
                    recv_sem=recv_sem.at[peer],
                    device_id=plane(peer),
                    device_id_type=MESH,
                ).wait_recv()

            loop(peers - 1, one)

        def wait_send():
            loop(peers - 1, lambda i: remote((me + 1 + i) % peers).wait_send())

        return wait_recv, wait_send

    by_source = lambda d: d
    by_member = lambda d: (d % members) * dp + d // members
    x_recv, x_sent = exchange(x_send, xr, x_ss, x_rs, by_source, load_sem.at[2])
    g_recv, g_sent = exchange(g_send, gr, g_ss, g_rs, by_source, load_sem.at[3])

    th = tile_of(hidden, 384)
    td = tile_of(width, 256)
    load1.wait()
    x_recv()

    def first_layer(j):
        cols = pl.ds(pl.multiple_of(j * th, 128), th)
        value, grad = gelu_pair(dot(xr[...].reshape(rows, width), w1[:, cols], 1, 0))
        act[:, cols] = value.astype(jnp.bfloat16)
        slope[:, cols] = grad

    loop(hidden // th, first_layer)
    load2.wait()

    def out_part(j):
        cols = pl.ds(pl.multiple_of(j * td, 128), td)
        part = dot(act[...], w2[:, cols], 1, 0).astype(jnp.bfloat16)
        po[:, :, cols] = part.reshape(peers, cap, td)

    loop(width // td, out_part)
    o_recv, o_sent = exchange(po, ro, o_ss, o_rs, by_member, load_sem.at[4])

    g_recv()

    def hidden_grad(j):
        cols = pl.ds(pl.multiple_of(j * th, 128), th)
        value = dot(gr[...].reshape(rows, width), w2[cols, :], 1, 1) * slope[:, cols]
        pg[:, cols] = value.astype(jnp.bfloat16)

    loop(hidden // th, hidden_grad)

    def dx_part(j):
        cols = pl.ds(pl.multiple_of(j * td, 128), td)
        part = dot(pg[...], w1[cols, :], 1, 1).astype(jnp.bfloat16)
        pd[:, :, cols] = part.reshape(peers, cap, td)

    loop(width // td, dx_part)
    d_recv, d_sent = exchange(pd, rd, d_ss, d_rs, by_member, load_sem.at[5])

    def weight_grads(j):
        cols = pl.ds(pl.multiple_of(j * td, 128), td)
        second[:, cols] = dot(act[...], gr[:, :, cols].reshape(rows, td), 0, 0).astype(jnp.bfloat16)
        first[cols, :] = dot(xr[:, :, cols].reshape(rows, td), pg[...], 0, 0).astype(jnp.bfloat16)

    loop(width // td, weight_grads)
    store1 = pltpu.make_async_copy(first, first_hbm, load_sem.at[0])
    store2 = pltpu.make_async_copy(second, second_hbm, load_sem.at[1])
    store1.start()
    store2.start()

    o_recv()
    router_part[...] = jnp.zeros_like(router_part)
    for m in range(members):
        part = dot(unperm[m], ro[m * dp : (m + 1) * dp].reshape(dp * cap, width), 1, 0)
        own[m * toks : (m + 1) * toks, :] = part.astype(jnp.bfloat16)
        gate_grad = jnp.sum(out_grad[m].astype(jnp.float32) * part, axis=-1, keepdims=True)
        weighted = tokens[...].astype(jnp.float32) * (gate_grad * gate_slope[m])
        router_part[...] += dot(hot_rows[m], weighted, 1, 0, lax.Precision.HIGHEST)

    def router_copy(z_to, z_from):
        return pltpu.make_async_remote_copy(
            src_ref=router_part,
            dst_ref=router_z.at[z_from],
            send_sem=rz_ss.at[z_to],
            recv_sem=rz_rs.at[z_from],
            device_id={"expert": z_to},
            device_id_type=MESH,
        )

    loop(zn - 1, lambda i: router_copy((me_z + 1 + i) % zn, me_z).start())
    router_z[me_z] = router_part[...]

    router_sends = []

    def finish_dx_and_router():
        d_recv()
        total = jnp.zeros((toks, width), jnp.float32)
        for m in range(members):
            total += dot(unperm[m], rd[m * dp : (m + 1) * dp].reshape(dp * cap, width), 1, 0)
        own[members * toks : (members + 1) * toks, :] = total.astype(jnp.bfloat16)
        loop(zn - 1, lambda i: router_copy((me_z + 1 + i) % zn, (me_z + 1 + i) % zn).wait_recv())
        router_sum[...] = jnp.sum(router_z[...], axis=0)
        loop(peers - 1, lambda i: router_plane((me + 1 + i) % peers, me).start())
        pltpu.make_async_copy(router_sum, router_all.at[me], load_sem.at[6]).start()

    def router_plane(to, slot):
        return pltpu.make_async_remote_copy(
            src_ref=router_sum,
            dst_ref=router_all.at[slot],
            send_sem=rp_ss.at[to],
            recv_sem=rp_rs.at[slot],
            device_id=plane(to),
            device_id_type=MESH,
        )

    mid = zn // 2 - 1
    left = me_z < zn // 2
    pos = jnp.where(left, me_z, zn - 1 - me_z)
    inner = jnp.where(left, me_z + 1, me_z - 1)
    outer = jnp.where(left, me_z - 1, me_z + 1)
    total_rows = (members + 1) * toks
    chunks = total_rows // chunk
    dx_chunk = members * toks // chunk

    def piece(k):
        return pl.ds(pl.multiple_of(k * chunk, chunk), chunk)

    def line(source, target, send_sem, recv_sem, k, z_to):
        return pltpu.make_async_remote_copy(
            src_ref=source.at[piece(k)],
            dst_ref=target.at[piece(k)],
            send_sem=send_sem.at[k],
            recv_sem=recv_sem.at[k],
            device_id={"expert": z_to},
            device_id_type=MESH,
        )

    def step(t):
        ka = t - pos
        kb = t - (2 * mid + 1 - pos)

        @pl.when((kb >= 0) & (kb < chunks))
        def _():
            @pl.when(pos == mid)
            def _():
                line(own, xch, xch_ss, xch_rs, kb, inner).wait()
                res[piece(kb), :] = (
                    own[piece(kb), :].astype(jnp.float32) + xch[piece(kb), :].astype(jnp.float32)
                ).astype(jnp.bfloat16)

            @pl.when(pos < mid)
            def _():
                line(res, res, res_ss, res_rs, kb, inner).wait_recv()

            @pl.when(pos > 0)
            def _():
                line(res, res, res_ss, res_rs, kb, outer).start()

        @pl.when(ka == dx_chunk)
        def _():
            finish_dx_and_router()

        @pl.when((ka >= 0) & (ka < chunks))
        def _():
            @pl.when(pos > 0)
            def _():
                line(own, red, red_ss, red_rs, ka, outer).wait_recv()
                own[piece(ka), :] = (
                    own[piece(ka), :].astype(jnp.float32) + red[piece(ka), :].astype(jnp.float32)
                ).astype(jnp.bfloat16)

            @pl.when(pos < mid)
            def _():
                line(own, red, red_ss, red_rs, ka, inner).start()

            @pl.when(pos == mid)
            def _():
                line(own, xch, xch_ss, xch_rs, ka, inner).start()

    loop(chunks + 2 * mid + 1, step)

    def drain(k):
        @pl.when(pos < mid)
        def _():
            line(own, red, red_ss, red_rs, k, inner).wait_send()

        @pl.when(pos > 0)
        def _():
            line(res, res, res_ss, res_rs, k, outer).wait_send()

    out_tot[...] = res[: members * toks, :]
    dx_tot[...] = res[members * toks :, :]
    loop(chunks, drain)
    x_sent()
    g_sent()
    o_sent()
    d_sent()
    store1.wait()
    store2.wait()
    loop(zn - 1, lambda i: router_copy((me_z + 1 + i) % zn, me_z).wait_send())
    loop(peers - 1, lambda i: router_plane((me + 1 + i) % peers, me).wait_send())
    loop(peers - 1, lambda i: router_plane((me + 1 + i) % peers, (me + 1 + i) % peers).wait_recv())
    pltpu.make_async_copy(router_sum, router_all.at[me], load_sem.at[6]).wait()


def shards(tokens, route_ids, router, w_in, w_out, out_grad):
    members, toks = route_ids.shape[:2]
    experts, width = router.shape[2], tokens.shape[1]
    dp, zn = lax.axis_size("dp"), lax.axis_size("expert")
    peers = dp * members
    hidden = w_in.shape[3]
    capacity = max(2, 3 * toks // (2 * experts))
    cap = -(-capacity // 16) * 16
    rows = peers * cap
    chunk = 32

    expert_ids = route_ids[:, :, 0]
    slots = slot_rank(expert_ids, experts)
    expert_range = jnp.arange(experts, dtype=jnp.int32)
    hot = expert_ids[..., None] == expert_range
    hot_f = hot.astype(jnp.float32)
    tokens_f = tokens.astype(jnp.float32)
    logits = jnp.einsum("td,mde->mte", tokens_f, router, precision=lax.Precision.HIGHEST)
    gate = jax.nn.sigmoid(jnp.sum(logits * hot_f, axis=-1))
    scaled = (gate[..., None] * out_grad.astype(jnp.float32)).astype(jnp.bfloat16)
    gate_slope = (gate * (1.0 - gate))[..., None]

    place = expert_ids * cap + slots
    unperm = (place[..., None] == jnp.arange(experts * cap, dtype=jnp.int32)).astype(jnp.bfloat16)
    member_range = jnp.arange(members, dtype=jnp.int32)[:, None]
    send_place = ((expert_ids * members + member_range) * cap + slots).reshape(1, -1)
    pick = (jnp.arange(rows, dtype=jnp.int32)[:, None] == send_place).astype(jnp.bfloat16)
    token_pick = (
        jnp.sum(pick.reshape(rows, members, toks).astype(jnp.float32), axis=1)
    ).astype(jnp.bfloat16)
    x_send = jnp.dot(token_pick, tokens, preferred_element_type=jnp.bfloat16)
    g_send = jnp.dot(pick, scaled.reshape(-1, width), preferred_element_type=jnp.bfloat16)
    hot_rows = (
        (member_range[:, :, None] == member_range[None, :, :])[..., None]
        & jnp.swapaxes(hot, 1, 2)[:, None]
    ).astype(jnp.float32).reshape(members, members * experts, toks)

    bf, f32 = jnp.bfloat16, jnp.float32
    vmem, anywhere = pl.BlockSpec(memory_space=pltpu.VMEM), pl.BlockSpec(memory_space=pl.ANY)
    total_rows = (members + 1) * toks
    chunks = total_rows // chunk
    dma = pltpu.SemaphoreType.DMA
    block = pltpu.VMEM((peers, cap, width), bf)
    line = pltpu.VMEM((total_rows, width), bf)
    router_shape = (members * experts, width)
    out_tot, dx_tot, first, second, router_all = pl.pallas_call(
        functools.partial(layer_kernel, (dp, members, zn, cap, toks, chunk)),
        out_shape=(
            jax.ShapeDtypeStruct((members * toks, width), bf),
            jax.ShapeDtypeStruct((toks, width), bf),
            jax.ShapeDtypeStruct((width, hidden), bf),
            jax.ShapeDtypeStruct((hidden, width), bf),
            jax.ShapeDtypeStruct((peers,) + router_shape, f32),
        ),
        in_specs=[vmem, vmem, anywhere, anywhere] + [vmem] * 5,
        out_specs=(vmem, vmem, anywhere, anywhere, anywhere),
        scratch_shapes=[
            pltpu.VMEM((width, hidden), bf),
            pltpu.VMEM((hidden, width), bf),
            block,
            block,
            pltpu.VMEM((rows, hidden), bf),
            pltpu.VMEM((rows, hidden), f32),
            pltpu.VMEM((rows, hidden), bf),
            block,
            block,
            block,
            block,
            pltpu.VMEM((width, hidden), bf),
            pltpu.VMEM((hidden, width), bf),
            line,
            line,
            line,
            line,
            pltpu.VMEM(router_shape, f32),
            pltpu.VMEM((zn,) + router_shape, f32),
            pltpu.VMEM(router_shape, f32),
            dma((7,)),
        ]
        + [dma((peers,))] * 8
        + [dma((chunks,))] * 6
        + [dma((zn,))] * 2
        + [dma((peers,))] * 2,
        compiler_params=pltpu.CompilerParams(
            collective_id=0, has_side_effects=True, vmem_limit_bytes=60 * 1024 * 1024
        ),
        cost_estimate=pl.CostEstimate(
            flops=12 * rows * width * hidden,
            bytes_accessed=8 * width * hidden,
            transcendentals=rows * hidden,
        ),
    )(
        x_send.reshape(peers, cap, width),
        g_send.reshape(peers, cap, width),
        w_in[0, 0],
        w_out[0, 0],
        unperm,
        tokens,
        out_grad,
        hot_rows,
        gate_slope,
    )

    output_f = out_tot.reshape(members, toks, width).astype(f32)
    moe_out = (gate[..., None] * output_f).astype(bf)
    gate_grad = jnp.sum(out_grad.astype(f32) * output_f, axis=-1)
    weighted = hot_f * (gate_grad[..., None] * gate_slope)
    router_term = jnp.einsum("mte,mde->td", weighted, router, precision=lax.Precision.HIGHEST)
    token_grad = router_term + dx_tot.astype(f32)
    router_grad = jnp.swapaxes(
        jnp.sum(router_all, axis=0).reshape(members, experts, width), 1, 2
    )
    return (moe_out, token_grad, first[None, None], second[None, None], router_grad)


def solution(mesh):
    in_specs = (
        P(("dp", "member"), None),
        P(None, ("dp", "member"), None),
        P(),
        P("member", "dp", None, "expert"),
        P("member", "dp", "expert", None),
        P(None, ("dp", "member"), None),
    )
    out_specs = (
        P(None, ("dp", "member"), None),
        P(("dp", "member"), None),
        P("member", "dp", None, "expert"),
        P("member", "dp", "expert", None),
        P(),
    )
    return jax.shard_map(shards, mesh=mesh, in_specs=in_specs, out_specs=out_specs, check_vma=False)
```

time: 218 us -> 118 us (0.54)
  waiting for transfers between devices: 110 us -> 0 us
  Pallas kernels: 0 us -> 97.1 us
  blocking collectives: 23.3 us -> 0 us
  starting transfers between devices: 18.1 us -> 0 us
  matrix products: 24.3 us -> 6.71 us
  between operations: 14.2 us -> 0.78 us
  local copies, waits for them, and re-layouts: 17.8 us -> 5.7 us
    pallas_call x0 -> x1, Pallas kernels: none -> 97.1 us  [shards(): pl.pallas_call(functools.partial(layer_kernel, (dp, members, zn, cap, tok...]
    psum x1 -> x0, waiting for transfers between devices: 82.2 us -> none  [block_sums(): lax.psum(first_part, 'expert').astype(jnp.float32)]
    all_to_all x4 -> x0, waiting for transfers between devices: 28.1 us -> none  [the longest x1 8.98 us: dispatch(): lax.all_to_all(x_send.reshape(experts * members, capacity, row_width), ('...]
    psum x1 -> x0, blocking collectives: 23.3 us -> none  [shards(): router_grad = lax.psum(router_local, ('dp', 'member'))]
    dot_general x7 -> x2, matrix products: 22.3 us -> 2.78 us  [the longest x1 1.42 us: shards(): jnp.dot(pick, scaled.reshape(-1, width), preferred_element_type=jnp.bfloa...]
    all_to_all x4 -> x0, starting transfers between devices: 18.1 us -> none  [the longest x1 5.17 us: dispatch(): lax.all_to_all(x_send.reshape(experts * members, capacity, row_width), ('...]
    gather x2 -> x0, local copies, waits for them, and re-layouts: 7.88 us -> none  [the longest x1 3.94 us: shards(): back_out[buffer_index].reshape(members, tok_rows, model_width)]
    scatter x2 -> x0, local copies, waits for them, and re-layouts: 6.53 us -> none  [the longest x1 3.28 us: shards(): g_send = jnp.zeros((total_rows, model_width), jnp.bfloat16).at[buffer_ind...]
  transfers between devices with their start and end apart: 5 -> 0, of which waited for: 5 -> 0; matrix products, arithmetic and copies ran while one was open for 13% -> 0% of each run, Pallas kernels for 0% -> 0%
where the time goes in v1:
time: 118 us
  Pallas kernels  97.1 us (82%)
  other arithmetic  7.45 us (6%)
  matrix products  6.71 us (6%)
  local copies, waits for them, and re-layouts  5.7 us (5%)
    pallas_call x1, Pallas kernels, shards(): pl.pallas_call(functools.partial(layer_kernel, (dp, members, zn, cap, tok...  97.1 us
    unnamed x18, local copies, waits for them, and re-layouts  4.54 us
    dot_general x1, matrix products, shards(): jnp.einsum('mte,mde->td', weighted, router, precision=lax.Precision.HIGHEST)  2.57 us

profile of v1, /device:TPU:0, one launch (start us, length us, event | category | flops | bytes accessed | tf_op | source)
XLA Modules:
  0.0 117.7 jit_solution(14508036315858740547)
XLA Ops:
  0.6 0.0 copy-start
  0.6 0.0 copy-start.3
  0.7 0.8 fusion.17
  1.4 0.1 copy.24
  1.6 0.2 reduce_window_sum.11
  1.7 0.1 copy.25
  1.8 0.7 select_reduce_fusion
  2.5 0.7 broadcast_multiply_fusion
  3.2 0.0 copy-done
  3.2 1.4 %fusion.5 = f32[2,128]{1,0:T(2,128)S(1)} fusion(f32[2,1280,4]{1,2,0:T(4,128)S(1)} %copy-done, bf16[128,1280]{1,0:T(8,128)(2,1)} %tokens.1, s32[2,128]{1,0:T(2,128)} %bitcast.58), kind=kOutput, calls=%fused_computation.10 | convolution fusion | flops 15731456 | bytes 370688 | tf_op jit(solution)/shard_map/td,mde->mte/dot_general | solution.py:327
  4.6 0.0 copy-done.3
  4.6 0.0 copy-start.7
  4.6 0.0 copy-start.5
  4.7 0.2 fusion.1
  4.8 1.4 %fusion.7.g_send = bf16[8,48,1280]{2,1,0:T(8,128)(2,1)} fusion(bf16[256,1280,1]{1,0,2:T(8,128)(2,1)S(1)} %bitcast.53, s32[256]{0:T(256)S(1)} %bitcast_add_fusion.1, s32[8,48]{1,0:T(8,128)S(1)} %multiply_add_fusion), kind=kOutput, calls=%fused_computation.13 | convolution fusion | flops 251756544 | bytes 1640960 | tf_op jit(solution)/shard_map/dot_general | solution.py:341
  6.3 0.0 copy-done.7
  6.3 0.1 fusion.13
  6.3 0.0 copy-done.5
  6.3 1.4 %fusion.9.x_send = bf16[8,48,1280]{2,1,0:T(8,128)(2,1)} fusion(bf16[8,48,128]{2,1,0:T(8,128)(2,1)S(1)} %bitcast.55, bf16[128,1280]{1,0:T(8,128)(2,1)S(1)} %copy-done.5), kind=kOutput, calls=%fused_computation.15 | convolution fusion | flops 125829120 | bytes 1409024 | tf_op jit(solution)/shard_map/dot_general | solution.py:340
  7.7 0.8 fusion.12.unperm
  8.5 0.1 copy.29
  8.6 0.7 subtract_multiply_fusion.gate_slope
  9.3 0.1 and.20
  9.4 0.1 and.21
  9.5 0.7 and_convert_fusion.hot_rows
  10.2 97.1 %shard_map.101 = (bf16[256,1280]{1,0:T(8,128)(2,1)}, bf16[128,1280]{1,0:T(8,128)(2,1)}, bf16[1280,1152]{1,0:T(8,128)(2,1)}, bf16[1152,1280]{1,0:T(8,128)(2,1)}, f32[8,8,1280]{2,1,0:T(8,128)}) custom-call(bf16[8,48,1280]{2,1,0:T(8,128)(2,1)} %fusion.9.x_send, bf16[8,48,1280]{2,1,0:T(8,128)(2,1)} %fusion.7.g_send, bf16[1280,1152]{1,0:T(8,128)(2,1)} %bitcast.66, ...), custom_call_target="tpu_custom_call" | custom-call | flops 6794772480 | bytes 11796480 | tf_op jit(solution)/shard_map/pallas_call | solution.py:355
  107.2 0.0 copy-start.4
  107.3 0.0 copy-start.6
  107.3 0.0 copy-start.2
  107.3 1.7 %fusion.3 = f32[2,128]{1,0:T(2,128)S(1)} fusion(bf16[2,128,1280]{2,1,0:T(8,128)(2,1)} %bitcast.54, bf16[2,128,1280]{2,1,0:T(8,128)(2,1)} %out_grad.1), kind=kLoop, calls=%fused_computation.7 | loop fusion | flops 1310464 | bytes 1311744 | tf_op jit(solution)/shard_map/reduce_sum | solution.py:415
  109.0 2.6 %fusion = f32[128,1280]{1,0:T(8,128)} fusion(f32[2,1280,4]{1,2,0:T(4,128)S(1)} %copy-done, bf16[128,1280]{1,0:T(8,128)(2,1)} %get-tuple-element.11, f32[2,128]{1,0:T(2,128)S(1)} %fusion.21, s32[2,128]{1,0:T(2,128)S(1)} %bitcast.62), kind=kOutput, calls=%fused_computation.1 | convolution fusion | flops 16058368 | bytes 1026048 | tf_op jit(solution)/shard_map/mte,mde->td/dot_general | solution.py:417
  111.5 0.0 copy-done.4
  111.5 1.0 fusion.2
  112.6 0.0 copy-done.6
  112.6 0.6 reshape.134
  113.2 0.0 copy-done.2
  113.2 0.0 copy-start.1
  113.2 1.6 %copy.32 = bf16[1,1,1280,1152]{3,2,1,0:T(8,128)(2,1)} copy(bf16[1,1,1280,1152]{3,2,1,0:T(8,128)(2,1)S(1)} %bitcast.52) | data formatting | bytes 5898240
  114.8 1.3 %copy-done.1 = bf16[1152,1280]{1,0:T(8,128)(2,1)S(1)} copy-done((bf16[1152,1280]{1,0:T(8,128)(2,1)S(1)}, bf16[1152,1280]{1,0:T(8,128)(2,1)}, u32[]{:S(2)}) %copy-start.1) | copy-done | bytes 2949144
  116.1 1.6 %copy.33 = bf16[1,1,1152,1280]{3,2,1,0:T(8,128)(2,1)} copy(bf16[1,1,1152,1280]{3,2,1,0:T(8,128)(2,1)S(1)} %bitcast.51) | data formatting | bytes 5898240
  (11 shorter events, 0.1 us)
Async XLA Ops:
  0.6 2.6 %copy-start = (f32[2,1280,4]{1,2,0:T(4,128)S(1)}, f32[2,1280,4]{1,2,0:T(4,128)}, u32[]{:S(2)}) copy-start(f32[2,1280,4]{1,2,0:T(4,128)} %param.8) | copy-start | bytes 122884
  0.6 4.0 %copy-start.3 = (bf16[2,128,1280]{2,1,0:T(8,128)(2,1)S(1)}, bf16[2,128,1280]{2,1,0:T(8,128)(2,1)}, u32[]{:S(2)}) copy-start(bf16[2,128,1280]{2,1,0:T(8,128)(2,1)} %out_grad.1) | copy-start | bytes 1966084
  4.6 1.6 %copy-start.7 = (s32[2,128,1]{1,2,0:T(1,128)S(1)}, s32[2,128,1]{1,2,0:T(1,128)}, u32[]{:S(2)}) copy-start(s32[2,128,1]{1,2,0:T(1,128)} %param.7) | copy-start | bytes 3076
  4.6 1.7 %copy-start.5 = (bf16[128,1280]{1,0:T(8,128)(2,1)S(1)}, bf16[128,1280]{1,0:T(8,128)(2,1)}, u32[]{:S(2)}) copy-start(bf16[128,1280]{1,0:T(8,128)(2,1)} %tokens.1) | copy-start | bytes 983044
  107.2 4.3 %copy-start.4 = (bf16[256,1280]{1,0:T(8,128)(2,1)S(1)}, bf16[256,1280]{1,0:T(8,128)(2,1)}, u32[]{:S(2)}) copy-start(bf16[256,1280]{1,0:T(8,128)(2,1)} %get-tuple-element.10) | copy-start | bytes 1966084
  107.3 5.3 %copy-start.6 = (f32[8,8,1280]{2,1,0:T(8,128)S(1)}, f32[8,8,1280]{2,1,0:T(8,128)}, u32[]{:S(2)}) copy-start(f32[8,8,1280]{2,1,0:T(8,128)} %get-tuple-element.14) | copy-start | bytes 983044
  107.3 6.0 %copy-start.2 = (bf16[1280,1152]{1,0:T(8,128)(2,1)S(1)}, bf16[1280,1152]{1,0:T(8,128)(2,1)}, u32[]{:S(2)}) copy-start(bf16[1280,1152]{1,0:T(8,128)(2,1)} %get-tuple-element.12) | copy-start | bytes 8847364
  113.2 2.9 %copy-start.1 = (bf16[1152,1280]{1,0:T(8,128)(2,1)S(1)}, bf16[1152,1280]{1,0:T(8,128)(2,1)}, u32[]{:S(2)}) copy-start(bf16[1152,1280]{1,0:T(8,128)(2,1)} %get-tuple-element.13) | copy-start | bytes 8847364

commit v2 on v1

v2 whole, which is shorter than its diff:
```python
import functools

import jax
import jax.numpy as jnp
from jax import lax
from jax.experimental import pallas as pl
from jax.experimental.pallas import tpu as pltpu
from jax.sharding import PartitionSpec as P

MESH = pl.DeviceIdType.MESH
tanh_scale = 0.7978845608028654
cubic_term = 0.044715


def gelu_pair(pre_act):
    square = pre_act * pre_act
    tanh_value = jnp.tanh(tanh_scale * (pre_act + cubic_term * square * pre_act))
    half = 0.5 * (1.0 + tanh_value)
    slope = half + 0.5 * pre_act * (1.0 - tanh_value * tanh_value) * tanh_scale * (
        1.0 + 3.0 * cubic_term * square
    )
    return pre_act * half, slope


def slot_rank(expert_ids, experts):
    hot_table = (expert_ids[..., None] == jnp.arange(experts, dtype=jnp.int32)).astype(jnp.int32)
    earlier = jnp.cumsum(hot_table, axis=-2) - hot_table
    return jnp.sum(earlier * hot_table, axis=-1)


def dot(a, b, ca, cb, precision=None):
    return lax.dot_general(
        a, b, (((ca,), (cb,)), ((), ())), precision=precision, preferred_element_type=jnp.float32
    )


def tile_of(size, wanted):
    while size % wanted:
        wanted -= 128
    return wanted


def layer_kernel(
    cfg,
    row_place, col_place, row_ids, col_ids, tokens, out_grad, router_t, w1_hbm, w2_hbm,
    moe_out, token_grad, first_hbm, second_hbm, router_all,
    x_send, g_send, picks, unperm, picked_router, gates, gate_grads,
    w1, w2, xr, gr, act, slope, pg, po, pd, ro, rd, first, second,
    own, red, xch, res, router_part, router_z, router_sum,
    load_sem, x_ss, x_rs, g_ss, g_rs, xf_ss, xf_rs, gf_ss, gf_rs, o_ss, o_rs, d_ss, d_rs,
    red_ss, red_rs, xch_ss, xch_rs, res_ss, res_rs, rz_ss, rz_rs, rp_ss, rp_rs,
):
    dp, members, zn, cap, toks, chunk = cfg
    peers = dp * members
    me_dp, me_m, me_z = lax.axis_index("dp"), lax.axis_index("member"), lax.axis_index("expert")
    me = me_dp * members + me_m
    width = x_send.shape[-1]
    half = width // 2
    hidden = w1.shape[1]
    rows = peers * cap
    experts = router_t.shape[1]
    bf, f32 = jnp.bfloat16, jnp.float32

    def plane(index):
        return {"dp": index // members, "member": index % members}

    def loop(count, body):
        lax.fori_loop(0, count, lambda i, c: (body(i), c)[1], 0)

    def each_peer(body):
        loop(peers - 1, lambda i: body((me + 1 + i) % peers))

    def each_z(body):
        loop(zn - 1, lambda i: body((me_z + 1 + i) % zn))

    def remote(source, target, send_sem, recv_sem, where):
        return pltpu.make_async_remote_copy(
            src_ref=source,
            dst_ref=target,
            send_sem=send_sem,
            recv_sem=recv_sem,
            device_id=where,
            device_id_type=MESH,
        )

    barrier = pltpu.get_barrier_semaphore()
    each_peer(
        lambda p: pl.semaphore_signal(barrier, inc=1, device_id=plane(p), device_id_type=MESH)
    )
    each_z(
        lambda z: pl.semaphore_signal(barrier, inc=1, device_id={"expert": z}, device_id_type=MESH)
    )
    load1 = pltpu.make_async_copy(w1_hbm, w1, load_sem.at[0])
    load2 = pltpu.make_async_copy(w2_hbm, w2, load_sem.at[1])
    load1.start()
    load2.start()

    relay = cap % 48 == 0
    third = cap // 3
    parity = me_z % 2
    partner = me_z + 1 - 2 * parity
    if relay:
        sent = pl.ds(pl.multiple_of(parity * third, 16), 2 * third)
        handed = pl.ds(pl.multiple_of(parity * 2 * third, 16), third)
        taken = pl.ds(pl.multiple_of((1 - parity) * 2 * third, 16), third)
    else:
        sent = pl.ds(0, cap)

    def dispatch(source, target, send_sem, recv_sem, relay_ss, relay_rs, own_sem):
        def send(peer, slot):
            return remote(
                source.at[peer, sent], target.at[slot, sent], send_sem.at[peer], recv_sem.at[slot], plane(peer)
            )

        def hand(peer, part):
            return remote(
                target.at[peer, part],
                target.at[peer, part],
                relay_ss.at[peer],
                relay_rs.at[peer],
                {"expert": partner},
            )

        mine = pltpu.make_async_copy(source.at[me], target.at[me], own_sem)

        def start():
            each_peer(lambda p: send(p, me).start())
            mine.start()

        def receive():
            def one(p):
                send(p, p).wait_recv()
                if relay:
                    hand(p, handed).start()

            each_peer(one)
            if relay:
                each_peer(lambda p: hand(p, taken).wait_recv())
            mine.wait()

        def finish():
            each_peer(lambda p: send(p, me).wait_send())
            if relay:
                each_peer(lambda p: hand(p, handed).wait_send())

        return start, receive, finish

    x_start, x_receive, x_finish = dispatch(x_send, xr, x_ss, x_rs, xf_ss, xf_rs, load_sem.at[2])
    g_start, g_receive, g_finish = dispatch(g_send, gr, g_ss, g_rs, gf_ss, gf_rs, load_sem.at[3])

    th = tile_of(hidden, 384)
    td = tile_of(width, 256)

    row_index = lax.broadcasted_iota(jnp.int32, (rows, toks), 0)
    for m in range(members):
        picks[m] = (row_index == row_place[m]).astype(f32).astype(bf)

    def pack_tokens(j):
        cols = pl.ds(pl.multiple_of(j * td, 128), td)
        value = sum(dot(picks[m], tokens[:, cols], 1, 0) for m in range(members))
        x_send[:, :, cols] = value.astype(bf).reshape(peers, cap, td)

    loop(width // td, pack_tokens)
    pl.semaphore_wait(barrier, peers + zn - 2)
    x_start()

    hot_index = lax.broadcasted_iota(jnp.int32, (toks, experts), 1)
    tokens_f = tokens[...].astype(f32)
    for m in range(members):
        hot = (hot_index == col_ids[m]).astype(f32)
        picked_router[m] = dot(hot, router_t[m], 1, 0, lax.Precision.HIGHEST)
        logit = jnp.sum(tokens_f * picked_router[m], axis=-1, keepdims=True)
        gates[m] = 1.0 / (1.0 + jnp.exp(-logit))

    def pack_grads(j):
        cols = pl.ds(pl.multiple_of(j * td, 128), td)
        value = sum(
            dot(picks[m], (gates[m] * out_grad[m, :, cols].astype(f32)).astype(bf), 1, 0)
            for m in range(members)
        )
        g_send[:, :, cols] = value.astype(bf).reshape(peers, cap, td)

    loop(width // td, pack_grads)
    g_start()
    place_index = lax.broadcasted_iota(jnp.int32, (toks, dp * cap), 1)
    for m in range(members):
        unperm[m] = (place_index == col_place[m]).astype(f32).astype(bf)

    load1.wait()
    x_receive()

    def first_layer(j):
        cols = pl.ds(pl.multiple_of(j * th, 128), th)
        value, grad = gelu_pair(dot(xr[...].reshape(rows, width), w1[:, cols], 1, 0))
        act[:, cols] = value.astype(bf)
        slope[:, cols] = grad

    loop(hidden // th, first_layer)
    load2.wait()

    by_member = lambda d: (d % members) * dp + d // members

    def give_back(source, target, send_sem, recv_sem, h, own_sem):
        def send(peer, sender):
            return remote(
                source.at[h, peer],
                target.at[h, by_member(sender)],
                send_sem.at[h, peer],
                recv_sem.at[h, sender],
                plane(peer),
            )

        mine = pltpu.make_async_copy(source.at[h, me], target.at[h, by_member(me)], own_sem)

        def start():
            each_peer(lambda p: send(p, me).start())
            mine.start()

        def receive():
            each_peer(lambda p: send(p, p).wait_recv())
            mine.wait()

        return start, receive, lambda: each_peer(lambda p: send(p, me).wait_send())

    outs = [give_back(po, ro, o_ss, o_rs, h, load_sem.at[4 + h]) for h in range(2)]
    dxs = [give_back(pd, rd, d_ss, d_rs, h, load_sem.at[6 + h]) for h in range(2)]

    for h in range(2):
        part = dot(act[...], w2[:, h * half : (h + 1) * half], 1, 0).astype(bf)
        po[h] = part.reshape(peers, cap, half)
        outs[h][0]()

    g_receive()

    def hidden_grad(j):
        cols = pl.ds(pl.multiple_of(j * th, 128), th)
        value = dot(gr[...].reshape(rows, width), w2[cols, :], 1, 1) * slope[:, cols]
        pg[:, cols] = value.astype(bf)

    loop(hidden // th, hidden_grad)
    for h in range(2):
        part = dot(pg[...], w1[h * half : (h + 1) * half, :], 1, 1).astype(bf)
        pd[h] = part.reshape(peers, cap, half)
        dxs[h][0]()

    mid = zn // 2 - 1
    left = me_z < zn // 2
    pos = jnp.where(left, me_z, zn - 1 - me_z)
    inner = jnp.where(left, me_z + 1, me_z - 1)
    outer = jnp.where(left, me_z - 1, me_z + 1)
    out_chunks = members * toks // chunk
    dx_chunks = toks // chunk
    chunks = 2 * (out_chunks + dx_chunks)
    per_member = toks // chunk
    lag = 2
    store1 = pltpu.make_async_copy(first, first_hbm, load_sem.at[0])
    store2 = pltpu.make_async_copy(second, second_hbm, load_sem.at[1])

    def router_copy(z_to, z_from):
        return remote(
            router_part, router_z.at[z_from], rz_ss.at[z_to], rz_rs.at[z_from], {"expert": z_to}
        )

    def router_plane(to, slot):
        return remote(router_sum, router_all.at[slot], rp_ss.at[to], rp_rs.at[slot], plane(to))

    router_mine = pltpu.make_async_copy(router_sum, router_all.at[me], load_sem.at[8])

    def second_grads(j):
        cols = pl.ds(pl.multiple_of(j * td, 128), td)
        second[:, cols] = dot(act[...], gr[:, :, cols].reshape(rows, td), 0, 0).astype(bf)

    def first_grads(j):
        cols = pl.ds(pl.multiple_of(j * td, 128), td)
        first[cols, :] = dot(xr[:, :, cols].reshape(rows, td), pg[...], 0, 0).astype(bf)

    def take_out(h):
        outs[h][1]()
        for m in range(members):
            part = dot(unperm[m], ro[h, m * dp : (m + 1) * dp].reshape(dp * cap, half), 1, 0)
            base = h * out_chunks + m * per_member
            own[base : base + per_member] = part.astype(bf).reshape(per_member, chunk, half)
            grad = out_grad[m, :, h * half : (h + 1) * half].astype(f32)
            partial = jnp.sum(grad * part, axis=-1, keepdims=True)
            gate_grads[m] = partial if h == 0 else gate_grads[m] + partial

    def send_router():
        total = jnp.zeros(router_part.shape, f32)
        hot_row = lax.broadcasted_iota(jnp.int32, (members * experts, toks), 0)
        for m in range(members):
            hot = (hot_row == row_ids[m] + m * experts).astype(f32)
            weight = gate_grads[m] * gates[m] * (1.0 - gates[m])
            total += dot(hot, tokens[...].astype(f32) * weight, 1, 0, lax.Precision.HIGHEST)
        router_part[...] = total
        each_z(lambda z: router_copy(z, me_z).start())
        router_z[me_z] = total

    def take_dx(h):
        dxs[h][1]()
        total = sum(
            dot(unperm[m], rd[h, m * dp : (m + 1) * dp].reshape(dp * cap, half), 1, 0)
            for m in range(members)
        )
        base = 2 * out_chunks + h * dx_chunks
        own[base : base + dx_chunks] = total.astype(bf).reshape(dx_chunks, chunk, half)

    def add_router():
        each_z(lambda z: router_copy(z, z).wait_recv())
        router_sum[...] = jnp.sum(router_z[...], axis=0)
        each_peer(lambda p: router_plane(p, me).start())
        router_mine.start()

    def line(source, target, send_sem, recv_sem, k, z_to):
        return remote(source.at[k], target.at[k], send_sem.at[k], recv_sem.at[k], {"expert": z_to})

    def step(t):
        ka = t - pos
        kb = t - (2 * mid + lag - pos)

        @pl.when((kb >= 0) & (kb < chunks))
        def _():
            @pl.when(pos == mid)
            def _():
                line(own, xch, xch_ss, xch_rs, kb, inner).wait()
                res[kb] = (own[kb].astype(f32) + xch[kb].astype(f32)).astype(bf)

            if mid > 1:

                @pl.when((pos < mid) & (pos > 0))
                def _():
                    line(res, res, res_ss, res_rs, kb, inner).wait_recv()

            @pl.when(pos > 0)
            def _():
                line(res, res, res_ss, res_rs, kb, outer).start()

        @pl.when(ka == 0)
        def _():
            take_out(0)

        @pl.when(ka == out_chunks)
        def _():
            loop(width // td, second_grads)
            store2.start()
            take_out(1)
            send_router()

        @pl.when(ka == 2 * out_chunks)
        def _():
            loop(width // td, first_grads)
            store1.start()
            add_router()
            take_dx(0)

        @pl.when(ka == 2 * out_chunks + dx_chunks)
        def _():
            take_dx(1)

        @pl.when((ka >= 0) & (ka < chunks))
        def _():
            @pl.when(pos > 0)
            def _():
                line(own, red, red_ss, red_rs, ka, outer).wait_recv()
                own[ka] = (own[ka].astype(f32) + red[ka].astype(f32)).astype(bf)

            @pl.when(pos < mid)
            def _():
                line(own, red, red_ss, red_rs, ka, inner).start()

            @pl.when(pos == mid)
            def _():
                line(own, xch, xch_ss, xch_rs, ka, inner).start()

    loop(chunks + 2 * mid + lag, step)

    def last_arrivals(k):
        @pl.when((pos < mid) & (pos == 0))
        def _():
            line(res, res, res_ss, res_rs, k, inner).wait_recv()

    loop(2 * out_chunks, last_arrivals)
    weights = []
    for m in range(members):
        total = jnp.zeros((toks, 1), f32)
        for h in range(2):
            cols = slice(h * half, (h + 1) * half)
            base = h * out_chunks + m * per_member
            value = res[base : base + per_member].reshape(toks, half).astype(f32)
            moe_out[m, :, cols] = (gates[m] * value).astype(bf)
            grad = out_grad[m, :, cols].astype(f32)
            total += jnp.sum(grad * value, axis=-1, keepdims=True)
        weights.append(total * gates[m] * (1.0 - gates[m]))
    loop(chunks - 2 * out_chunks, lambda k: last_arrivals(k + 2 * out_chunks))
    for h in range(2):
        cols = slice(h * half, (h + 1) * half)
        base = 2 * out_chunks + h * dx_chunks
        value = res[base : base + dx_chunks].reshape(toks, half).astype(f32)
        for m in range(members):
            value += weights[m] * picked_router[m, :, cols]
        token_grad[:, cols] = value

    def drain(k):
        @pl.when(pos < mid)
        def _():
            line(own, red, red_ss, red_rs, k, inner).wait_send()

        @pl.when(pos > 0)
        def _():
            line(res, res, res_ss, res_rs, k, outer).wait_send()

    loop(chunks, drain)
    x_finish()
    g_finish()
    for h in range(2):
        outs[h][2]()
        dxs[h][2]()
    store1.wait()
    store2.wait()
    each_z(lambda z: router_copy(z, me_z).wait_send())
    each_peer(lambda p: router_plane(p, me).wait_send())
    each_peer(lambda p: router_plane(p, p).wait_recv())
    router_mine.wait()


def shards(tokens, route_ids, router, w_in, w_out, out_grad):
    members, toks = route_ids.shape[:2]
    experts, width = router.shape[2], tokens.shape[1]
    dp, zn = lax.axis_size("dp"), lax.axis_size("expert")
    peers = dp * members
    hidden = w_in.shape[3]
    capacity = max(2, 3 * toks // (2 * experts))
    cap = -(-capacity // 16) * 16
    rows = peers * cap
    chunk = toks // 2
    half = width // 2
    bf, f32 = jnp.bfloat16, jnp.float32

    expert_ids = route_ids[:, :, 0]
    slots = slot_rank(expert_ids, experts)
    member_range = jnp.arange(members, dtype=jnp.int32)[:, None]
    col_place = expert_ids * cap + slots
    row_place = (expert_ids * members + member_range) * cap + slots

    vmem, anywhere = pl.BlockSpec(memory_space=pltpu.VMEM), pl.BlockSpec(memory_space=pl.ANY)
    chunks = 2 * (members + 1) * toks // chunk
    dma = pltpu.SemaphoreType.DMA
    block = pltpu.VMEM((peers, cap, width), bf)
    halves = pltpu.VMEM((2, peers, cap, half), bf)
    line = pltpu.VMEM((chunks, chunk, half), bf)
    router_shape = (members * experts, width)
    moe_out, token_grad, first, second, router_all = pl.pallas_call(
        functools.partial(layer_kernel, (dp, members, zn, cap, toks, chunk)),
        out_shape=(
            jax.ShapeDtypeStruct((members, toks, width), bf),
            jax.ShapeDtypeStruct((toks, width), f32),
            jax.ShapeDtypeStruct((width, hidden), bf),
            jax.ShapeDtypeStruct((hidden, width), bf),
            jax.ShapeDtypeStruct((peers,) + router_shape, f32),
        ),
        in_specs=[vmem] * 7 + [anywhere] * 2,
        out_specs=(vmem, vmem, anywhere, anywhere, anywhere),
        scratch_shapes=[
            block,
            block,
            pltpu.VMEM((members, rows, toks), bf),
            pltpu.VMEM((members, toks, dp * cap), bf),
            pltpu.VMEM((members, toks, width), f32),
            pltpu.VMEM((members, toks, 1), f32),
            pltpu.VMEM((members, toks, 1), f32),
            pltpu.VMEM((width, hidden), bf),
            pltpu.VMEM((hidden, width), bf),
            block,
            block,
            pltpu.VMEM((rows, hidden), bf),
            pltpu.VMEM((rows, hidden), f32),
            pltpu.VMEM((rows, hidden), bf),
            halves,
            halves,
            halves,
            halves,
            pltpu.VMEM((width, hidden), bf),
            pltpu.VMEM((hidden, width), bf),
            line,
            line,
            line,
            line,
            pltpu.VMEM(router_shape, f32),
            pltpu.VMEM((zn,) + router_shape, f32),
            pltpu.VMEM(router_shape, f32),
            dma((9,)),
        ]
        + [dma((peers,))] * 8
        + [dma((2, peers))] * 4
        + [dma((chunks,))] * 6
        + [dma((zn,))] * 2
        + [dma((peers,))] * 2,
        compiler_params=pltpu.CompilerParams(
            collective_id=0, has_side_effects=True, vmem_limit_bytes=60 * 1024 * 1024
        ),
        cost_estimate=pl.CostEstimate(
            flops=12 * rows * width * hidden,
            bytes_accessed=8 * width * hidden,
            transcendentals=rows * hidden,
        ),
    )(
        row_place[:, None, :],
        col_place[..., None],
        expert_ids[:, None, :],
        expert_ids[..., None],
        tokens,
        out_grad,
        jnp.swapaxes(router, 1, 2),
        w_in[0, 0],
        w_out[0, 0],
    )
    router_grad = jnp.swapaxes(
        jnp.sum(router_all, axis=0).reshape(members, experts, width), 1, 2
    )
    return (moe_out, token_grad, first[None, None], second[None, None], router_grad)


def solution(mesh):
    in_specs = (
        P(("dp", "member"), None),
        P(None, ("dp", "member"), None),
        P(),
        P("member", "dp", None, "expert"),
        P("member", "dp", "expert", None),
        P(None, ("dp", "member"), None),
    )
    out_specs = (
        P(None, ("dp", "member"), None),
        P(("dp", "member"), None),
        P("member", "dp", None, "expert"),
        P("member", "dp", "expert", None),
        P(),
    )
    return jax.shard_map(shards, mesh=mesh, in_specs=in_specs, out_specs=out_specs, check_vma=False)
```

time: 118 us -> 105 us (0.89)
  Pallas kernels: 97.1 us -> 87.4 us
  matrix products: 6.71 us -> 0 us
  local copies, waits for them, and re-layouts: 5.7 us -> 11.3 us
  other arithmetic: 7.45 us -> 4.91 us
    pallas_call x1, Pallas kernels: 97.1 us -> 87.4 us  [shards(): pl.pallas_call(functools.partial(layer_kernel, (dp, members, zn, cap, tok...]
    dot_general x4 -> x0, matrix products: 6.71 us -> none  [the longest x1 2.57 us: shards(): jnp.einsum('mte,mde->td', weighted, router, precision=lax.Precision.HIGHEST)]
    unnamed x18 -> x9, local copies, waits for them, and re-layouts: 4.54 us -> 9.9 us
    convert_element_type x4 -> x0, other arithmetic: 2.62 us -> none  [the longest x1 1.01 us: shards(): moe_out = (gate[..., None] * output_f).astype(bf)]
    add x2, other arithmetic: 0.02 us -> 1.93 us  [the longest x1 1.25 us: shards(): row_place = (expert_ids * members + member_range) * cap + slots]
    reduce_sum x2 -> x0, other arithmetic: 1.74 us -> none  [the longest x1 1.69 us: shards(): gate_grad = jnp.sum(out_grad.astype(f32) * output_f, axis=-1)]
    mul x3 -> x0, other arithmetic: 1.37 us -> none  [the longest x1 0.68 us: shards(): expert_ids * members + member_range]
where the time goes in v2:
time: 105 us; the launch traced here: 104 us
  Pallas kernels  87.4 us (83%)
  local copies, waits for them, and re-layouts  11.3 us (11%)
  other arithmetic  4.91 us (5%)
    pallas_call x1, Pallas kernels, shards(): pl.pallas_call(functools.partial(layer_kernel, (dp, members, zn, cap, tok...  87.4 us
    unnamed x9, local copies, waits for them, and re-layouts  9.9 us

profile of v2, /device:TPU:0, one launch (start us, length us, event | category | flops | bytes accessed | tf_op | source)
XLA Modules:
  0.0 104.3 jit_solution(18111506001014762337)
XLA Ops:
  0.6 0.8 fusion
  1.4 0.2 reduce_window_sum.11
  1.6 0.9 select_reduce_fusion
  2.5 1.3 %multiply_add_fusion.row_place = s32[2,1,128]{2,1,0:T(1,128)} fusion(s32[2,1,128]{2,1,0:T(1,128)S(1)} %bitcast.20, s32[2,128,1]{1,2,0:T(1,128)} %param.7), kind=kLoop, calls=%fused_computation.4 | loop fusion | flops 1024 | bytes 3072 | tf_op jit(solution)/shard_map/add | solution.py:442
  3.7 0.7 bitcast_add_fusion
  4.4 0.8 copy.12.col_place
  5.2 1.5 %copy.13.col_ids = s32[2,128,1]{2,1,0:T(8,128)} copy(s32[2,128,1]{1,2,0:T(1,128)} %param.7) | data formatting | bytes 2048 | tf_op args[1]
  6.7 87.4 %shard_map.101 = (bf16[2,128,1280]{2,1,0:T(8,128)(2,1)}, f32[128,1280]{1,0:T(8,128)}, bf16[1280,1152]{1,0:T(8,128)(2,1)}, bf16[1152,1280]{1,0:T(8,128)(2,1)}, f32[8,8,1280]{2,1,0:T(8,128)}) custom-call(s32[2,1,128]{2,1,0:T(1,128)} %multiply_add_fusion.row_place, s32[2,128,1]{2,1,0:T(8,128)} %copy.12.col_place, s32[2,1,128]{2,1,0:T(1,128)} %bitcast.19, ...), custom_call_target="tpu_custom_call" | custom-call | flops 6794772480 | bytes 11796480 | tf_op jit(solution)/shard_map/pallas_call | solution.py:451
  94.1 0.0 copy-start.1
  94.1 1.1 %reduce_sum.25 = f32[8,1280]{1,0:T(8,128)S(1)} reduce(f32[8,8,1280]{2,1,0:T(8,128)} %get-tuple-element.14, f32[]{:T(128)} %constant.11.clone.1), dimensions={0}, to_apply=%region_2.3 | reduce | flops 71680 | bytes 368644 | tf_op jit(solution)/shard_map/reduce_sum | solution.py:517
  95.2 0.6 reshape.43
  95.8 2.0 %copy.18 = bf16[2,128,1280]{2,1,0:T(8,128)(2,1)} copy(bf16[2,128,1280]{2,1,0:T(8,128)(2,1)} %get-tuple-element.20) | data formatting | bytes 1310720
  97.8 2.0 %copy.19 = f32[128,1280]{1,0:T(8,128)} copy(f32[128,1280]{1,0:T(8,128)} %get-tuple-element.21) | data formatting | bytes 1310720
  99.8 0.0 copy-done.1
  99.8 0.0 copy-start
  99.8 1.6 %copy.20 = bf16[1,1,1280,1152]{3,2,1,0:T(8,128)(2,1)} copy(bf16[1,1,1280,1152]{3,2,1,0:T(8,128)(2,1)S(1)} %bitcast.14) | data formatting | bytes 5898240
  101.4 1.3 %copy-done = bf16[1152,1280]{1,0:T(8,128)(2,1)S(1)} copy-done((bf16[1152,1280]{1,0:T(8,128)(2,1)S(1)}, bf16[1152,1280]{1,0:T(8,128)(2,1)}, u32[]{:S(2)}) %copy-start) | copy-done | bytes 2949144
  102.7 1.6 %copy.21 = bf16[1,1,1152,1280]{3,2,1,0:T(8,128)(2,1)} copy(bf16[1,1,1152,1280]{3,2,1,0:T(8,128)(2,1)S(1)} %bitcast.13) | data formatting | bytes 5898240
Async XLA Ops:
  94.1 5.7 %copy-start.1 = (bf16[1280,1152]{1,0:T(8,128)(2,1)S(1)}, bf16[1280,1152]{1,0:T(8,128)(2,1)}, u32[]{:S(2)}) copy-start(bf16[1280,1152]{1,0:T(8,128)(2,1)} %get-tuple-element.12) | copy-start | bytes 8847364
  99.8 2.9 %copy-start = (bf16[1152,1280]{1,0:T(8,128)(2,1)S(1)}, bf16[1152,1280]{1,0:T(8,128)(2,1)}, u32[]{:S(2)}) copy-start(bf16[1152,1280]{1,0:T(8,128)(2,1)} %get-tuple-element.13) | copy-start | bytes 8847364

commit v3 on v2

--- a/solution.py
+++ b/solution.py
@@ -22,12 +22,6 @@
     return pre_act * half, slope
 
 
-def slot_rank(expert_ids, experts):
-    hot_table = (expert_ids[..., None] == jnp.arange(experts, dtype=jnp.int32)).astype(jnp.int32)
-    earlier = jnp.cumsum(hot_table, axis=-2) - hot_table
-    return jnp.sum(earlier * hot_table, axis=-1)
-
-
 def dot(a, b, ca, cb, precision=None):
     return lax.dot_general(
         a, b, (((ca,), (cb,)), ((), ())), precision=precision, preferred_element_type=jnp.float32
@@ -42,7 +36,7 @@
 
 def layer_kernel(
     cfg,
-    row_place, col_place, row_ids, col_ids, tokens, out_grad, router_t, w1_hbm, w2_hbm,
+    row_ids, tokens, out_grad, router_t, w1_hbm, w2_hbm,
     moe_out, token_grad, first_hbm, second_hbm, router_all,
     x_send, g_send, picks, unperm, picked_router, gates, gate_grads,
     w1, w2, xr, gr, act, slope, pg, po, pd, ro, rd, first, second,
@@ -67,8 +61,16 @@
     def loop(count, body):
         lax.fori_loop(0, count, lambda i, c: (body(i), c)[1], 0)
 
+    def flipped(index, bits):
+        places = range(peers.bit_length() - 1)
+        return sum(((index // (1 << b) + bits // (1 << b)) % 2) * (1 << b) for b in places)
+
     def each_peer(body):
-        loop(peers - 1, lambda i: body((me + 1 + i) % peers))
+        if peers & (peers - 1):
+            loop(peers - 1, lambda i: body((me + 1 + i) % peers))
+        else:
+            turn = (peers // 2 - 1) * me_m
+            loop(peers - 1, lambda i: body(flipped(me, (i + 1 + turn) % peers + (i + 1 + turn) // peers)))
 
     def each_z(body):
         loop(zn - 1, lambda i: body((me_z + 1 + i) % zn))
@@ -127,13 +129,15 @@
             each_peer(lambda p: send(p, me).start())
             mine.start()
 
-        def receive():
+        def receive(then=None):
             def one(p):
                 send(p, p).wait_recv()
                 if relay:
                     hand(p, handed).start()
 
             each_peer(one)
+            if then is not None:
+                then()
             if relay:
                 each_peer(lambda p: hand(p, taken).wait_recv())
             mine.wait()
@@ -151,9 +155,21 @@
     th = tile_of(hidden, 384)
     td = tile_of(width, 256)
 
-    row_index = lax.broadcasted_iota(jnp.int32, (rows, toks), 0)
+    def count_up(shape, axis):
+        return lax.broadcasted_iota(jnp.int32, shape, axis).astype(f32)
+
+    down, across = count_up((toks, toks), 0), count_up((toks, toks), 1)
+    row_index = count_up((rows, toks), 0)
+    col_ids, col_slot = [], []
     for m in range(members):
-        picks[m] = (row_index == row_place[m]).astype(f32).astype(bf)
+        row_id = row_ids[m].astype(f32)
+        col_id = jnp.sum(jnp.where(down == across, row_id, 0.0), axis=1, keepdims=True)
+        same = (col_id == row_id).astype(f32)
+        row_slot = jnp.sum(jnp.where(down < across, same, 0.0), axis=0, keepdims=True)
+        col_slot.append(jnp.sum(jnp.where(across < down, same, 0.0), axis=1, keepdims=True))
+        col_ids.append(col_id)
+        row_place = (row_id * members + m) * cap + row_slot
+        picks[m] = (row_index == row_place).astype(f32).astype(bf)
 
     def pack_tokens(j):
         cols = pl.ds(pl.multiple_of(j * td, 128), td)
@@ -164,7 +180,7 @@
     pl.semaphore_wait(barrier, peers + zn - 2)
     x_start()
 
-    hot_index = lax.broadcasted_iota(jnp.int32, (toks, experts), 1)
+    hot_index = count_up((toks, experts), 1)
     tokens_f = tokens[...].astype(f32)
     for m in range(members):
         hot = (hot_index == col_ids[m]).astype(f32)
@@ -181,13 +197,12 @@
         g_send[:, :, cols] = value.astype(bf).reshape(peers, cap, td)
 
     loop(width // td, pack_grads)
-    g_start()
-    place_index = lax.broadcasted_iota(jnp.int32, (toks, dp * cap), 1)
+    place_index = count_up((toks, dp * cap), 1)
     for m in range(members):
-        unperm[m] = (place_index == col_place[m]).astype(f32).astype(bf)
+        unperm[m] = (place_index == col_ids[m] * cap + col_slot[m]).astype(f32).astype(bf)
 
     load1.wait()
-    x_receive()
+    x_receive(g_start)
 
     def first_layer(j):
         cols = pl.ds(pl.multiple_of(j * th, 128), th)
@@ -228,9 +243,10 @@
     for h in range(2):
         part = dot(act[...], w2[:, h * half : (h + 1) * half], 1, 0).astype(bf)
         po[h] = part.reshape(peers, cap, half)
-        outs[h][0]()
-
-    g_receive()
+        if h == 0:
+            outs[h][0]()
+
+    g_receive(outs[1][0])
 
     def hidden_grad(j):
         cols = pl.ds(pl.multiple_of(j * th, 128), th)
@@ -267,8 +283,8 @@
     router_mine = pltpu.make_async_copy(router_sum, router_all.at[me], load_sem.at[8])
 
     def second_grads(j):
-        cols = pl.ds(pl.multiple_of(j * td, 128), td)
-        second[:, cols] = dot(act[...], gr[:, :, cols].reshape(rows, td), 0, 0).astype(bf)
+        cols = pl.ds(pl.multiple_of(j * th, 128), th)
+        second[cols, :] = dot(act[:, cols], gr[...].reshape(rows, width), 0, 0).astype(bf)
 
     def first_grads(j):
         cols = pl.ds(pl.multiple_of(j * td, 128), td)
@@ -340,7 +356,7 @@
 
         @pl.when(ka == out_chunks)
         def _():
-            loop(width // td, second_grads)
+            loop(hidden // th, second_grads)
             store2.start()
             take_out(1)
             send_router()
@@ -422,6 +438,28 @@
     router_mine.wait()
 
 
+parts = 4
+
+
+def write_out(moe, grad, first, second, routers, moe_to, grad_to, first_to, second_to, router_to, sem):
+    copies = []
+    for source, target in ((first, first_to), (second, second_to)):
+        size = source.shape[0] // parts
+        for k in range(parts):
+            piece = pl.ds(k * size, size)
+            copies.append((source.at[piece], target.at[piece]))
+    copies += [(moe, moe_to), (grad, grad_to)]
+    copies = [pltpu.make_async_copy(a, b, sem.at[k]) for k, (a, b) in enumerate(copies)]
+    for copy in copies:
+        copy.start()
+    total = jnp.sum(routers[...], axis=0)
+    members, experts = router_to.shape[:2]
+    for m in range(members):
+        router_to[m] = total[m * experts : (m + 1) * experts]
+    for copy in copies:
+        copy.wait()
+
+
 def shards(tokens, route_ids, router, w_in, w_out, out_grad):
     members, toks = route_ids.shape[:2]
     experts, width = router.shape[2], tokens.shape[1]
@@ -431,15 +469,9 @@
     capacity = max(2, 3 * toks // (2 * experts))
     cap = -(-capacity // 16) * 16
     rows = peers * cap
-    chunk = toks // 2
+    chunk = toks // 4
     half = width // 2
     bf, f32 = jnp.bfloat16, jnp.float32
-
-    expert_ids = route_ids[:, :, 0]
-    slots = slot_rank(expert_ids, experts)
-    member_range = jnp.arange(members, dtype=jnp.int32)[:, None]
-    col_place = expert_ids * cap + slots
-    row_place = (expert_ids * members + member_range) * cap + slots
 
     vmem, anywhere = pl.BlockSpec(memory_space=pltpu.VMEM), pl.BlockSpec(memory_space=pl.ANY)
     chunks = 2 * (members + 1) * toks // chunk
@@ -457,7 +489,7 @@
             jax.ShapeDtypeStruct((hidden, width), bf),
             jax.ShapeDtypeStruct((peers,) + router_shape, f32),
         ),
-        in_specs=[vmem] * 7 + [anywhere] * 2,
+        in_specs=[vmem] * 4 + [anywhere] * 2,
         out_specs=(vmem, vmem, anywhere, anywhere, anywhere),
         scratch_shapes=[
             block,
@@ -503,19 +535,24 @@
             transcendentals=rows * hidden,
         ),
     )(
-        row_place[:, None, :],
-        col_place[..., None],
-        expert_ids[:, None, :],
-        expert_ids[..., None],
+        jnp.swapaxes(route_ids, 1, 2),
         tokens,
         out_grad,
         jnp.swapaxes(router, 1, 2),
         w_in[0, 0],
         w_out[0, 0],
     )
-    router_grad = jnp.swapaxes(
-        jnp.sum(router_all, axis=0).reshape(members, experts, width), 1, 2
-    )
+    finals = (moe_out, token_grad, first, second)
+    moe_out, token_grad, first, second, router_sum = pl.pallas_call(
+        write_out,
+        out_shape=tuple(jax.ShapeDtypeStruct(v.shape, v.dtype) for v in finals)
+        + (jax.ShapeDtypeStruct((members, experts, width), f32),),
+        in_specs=[anywhere] * 4 + [vmem],
+        out_specs=(anywhere,) * 4 + (vmem,),
+        scratch_shapes=[dma((2 + 2 * parts,))],
+        compiler_params=pltpu.CompilerParams(vmem_limit_bytes=60 * 1024 * 1024),
+    )(*finals, router_all)
+    router_grad = jnp.swapaxes(router_sum, 1, 2)
     return (moe_out, token_grad, first[None, None], second[None, None], router_grad)
 
 

time: 105 us -> 323 us (3.08)
  Pallas kernels: 87.4 us -> 323 us
  local copies, waits for them, and re-layouts: 11.3 us -> 0 us
  other arithmetic: 4.91 us -> 0 us
    pallas_call x0 -> x1, Pallas kernels: none -> 221 us  [shards(): pl.pallas_call(write_out, out_shape=tuple((jax.ShapeDtypeStruct(v.shape,...]
    pallas_call x1, Pallas kernels: 87.4 us -> 101 us  [shards(): pl.pallas_call(functools.partial(layer_kernel, (dp, members, zn, cap, tok...]
    unnamed x9 -> x0, local copies, waits for them, and re-layouts: 9.9 us -> none
where the time goes in v3:
time: 323 us
  Pallas kernels  323 us (100%)
    pallas_call x1, Pallas kernels, shards(): pl.pallas_call(write_out, out_shape=tuple((jax.ShapeDtypeStruct(v.shape,...  221 us
    pallas_call x1, Pallas kernels, shards(): pl.pallas_call(functools.partial(layer_kernel, (dp, members, zn, cap, tok...  101 us

profile of v3, /device:TPU:0, one launch (start us, length us, event | category | flops | bytes accessed | tf_op | source)
XLA Modules:
  0.0 323.2 jit_solution(11527852137094485811)
XLA Ops:
  0.6 101.4 %shard_map.101 = (bf16[2,128,1280]{2,1,0:T(8,128)(2,1)}, f32[128,1280]{1,0:T(8,128)}, bf16[1280,1152]{1,0:T(8,128)(2,1)}, bf16[1152,1280]{1,0:T(8,128)(2,1)}, f32[8,8,1280]{2,1,0:T(8,128)}) custom-call(s32[2,1,128]{2,1,0:T(1,128)} %bitcast.13, bf16[128,1280]{1,0:T(8,128)(2,1)} %tokens.1, bf16[2,128,1280]{2,1,0:T(8,128)(2,1)} %out_grad.1, ...), custom_call_target="tpu_custom_call" | custom-call | flops 6794772480 | bytes 11796480 | tf_op jit(solution)/shard_map/pallas_call | solution.py:483
  102.0 221.2 %shard_map.102 = (bf16[2,128,1280]{2,1,0:T(8,128)(2,1)}, f32[128,1280]{1,0:T(8,128)}, bf16[1280,1152]{1,0:T(8,128)(2,1)}, bf16[1152,1280]{1,0:T(8,128)(2,1)}, f32[2,4,1280]{2,1,0:T(4,128)}) custom-call(bf16[2,128,1280]{2,1,0:T(8,128)(2,1)} %get-tuple-element.15.moe, f32[128,1280]{1,0:T(8,128)} %get-tuple-element.16.grad, ...), custom_call_target="tpu_custom_call" | custom-call | tf_op jit(solution)/shard_map/pallas_call | solution.py:546

commit v4 on v3

--- a/solution.py
+++ b/solution.py
@@ -61,16 +61,8 @@
     def loop(count, body):
         lax.fori_loop(0, count, lambda i, c: (body(i), c)[1], 0)
 
-    def flipped(index, bits):
-        places = range(peers.bit_length() - 1)
-        return sum(((index // (1 << b) + bits // (1 << b)) % 2) * (1 << b) for b in places)
-
     def each_peer(body):
-        if peers & (peers - 1):
-            loop(peers - 1, lambda i: body((me + 1 + i) % peers))
-        else:
-            turn = (peers // 2 - 1) * me_m
-            loop(peers - 1, lambda i: body(flipped(me, (i + 1 + turn) % peers + (i + 1 + turn) // peers)))
+        loop(peers - 1, lambda i: body((me + 1 + i) % peers))
 
     def each_z(body):
         loop(zn - 1, lambda i: body((me_z + 1 + i) % zn))
@@ -129,15 +121,13 @@
             each_peer(lambda p: send(p, me).start())
             mine.start()
 
-        def receive(then=None):
+        def receive():
             def one(p):
                 send(p, p).wait_recv()
                 if relay:
                     hand(p, handed).start()
 
             each_peer(one)
-            if then is not None:
-                then()
             if relay:
                 each_peer(lambda p: hand(p, taken).wait_recv())
             mine.wait()
@@ -197,12 +187,13 @@
         g_send[:, :, cols] = value.astype(bf).reshape(peers, cap, td)
 
     loop(width // td, pack_grads)
+    g_start()
     place_index = count_up((toks, dp * cap), 1)
     for m in range(members):
         unperm[m] = (place_index == col_ids[m] * cap + col_slot[m]).astype(f32).astype(bf)
 
     load1.wait()
-    x_receive(g_start)
+    x_receive()
 
     def first_layer(j):
         cols = pl.ds(pl.multiple_of(j * th, 128), th)
@@ -243,10 +234,9 @@
     for h in range(2):
         part = dot(act[...], w2[:, h * half : (h + 1) * half], 1, 0).astype(bf)
         po[h] = part.reshape(peers, cap, half)
-        if h == 0:
-            outs[h][0]()
-
-    g_receive(outs[1][0])
+        outs[h][0]()
+
+    g_receive()
 
     def hidden_grad(j):
         cols = pl.ds(pl.multiple_of(j * th, 128), th)
@@ -441,23 +431,18 @@
 parts = 4
 
 
-def write_out(moe, grad, first, second, routers, moe_to, grad_to, first_to, second_to, router_to, sem):
-    copies = []
-    for source, target in ((first, first_to), (second, second_to)):
-        size = source.shape[0] // parts
-        for k in range(parts):
-            piece = pl.ds(k * size, size)
-            copies.append((source.at[piece], target.at[piece]))
-    copies += [(moe, moe_to), (grad, grad_to)]
-    copies = [pltpu.make_async_copy(a, b, sem.at[k]) for k, (a, b) in enumerate(copies)]
-    for copy in copies:
-        copy.start()
-    total = jnp.sum(routers[...], axis=0)
-    members, experts = router_to.shape[:2]
-    for m in range(members):
-        router_to[m] = total[m * experts : (m + 1) * experts]
-    for copy in copies:
-        copy.wait()
+def write_out(moe, grad, first, second, routers, moe_to, grad_to, first_to, second_to, router_to):
+    moe_to[...] = moe[...]
+    grad_to[...] = grad[...]
+    first_to[...] = first[...]
+    second_to[...] = second[...]
+
+    @pl.when(pl.program_id(0) == 0)
+    def _():
+        total = jnp.sum(routers[...], axis=0)
+        members, experts = router_to.shape[:2]
+        for m in range(members):
+            router_to[m] = total[m * experts : (m + 1) * experts]
 
 
 def shards(tokens, route_ids, router, w_in, w_out, out_grad):
@@ -469,7 +454,7 @@
     capacity = max(2, 3 * toks // (2 * experts))
     cap = -(-capacity // 16) * 16
     rows = peers * cap
-    chunk = toks // 4
+    chunk = toks // 2
     half = width // 2
     bf, f32 = jnp.bfloat16, jnp.float32
 
@@ -543,13 +528,19 @@
         w_out[0, 0],
     )
     finals = (moe_out, token_grad, first, second)
+    pieces = [
+        pl.BlockSpec((members, toks // parts, width), lambda i: (0, i, 0)),
+        pl.BlockSpec((toks // parts, width), lambda i: (i, 0)),
+        pl.BlockSpec((width // parts, hidden), lambda i: (i, 0)),
+        pl.BlockSpec((hidden // parts, width), lambda i: (i, 0)),
+    ]
     moe_out, token_grad, first, second, router_sum = pl.pallas_call(
         write_out,
+        grid=(parts,),
         out_shape=tuple(jax.ShapeDtypeStruct(v.shape, v.dtype) for v in finals)
         + (jax.ShapeDtypeStruct((members, experts, width), f32),),
-        in_specs=[anywhere] * 4 + [vmem],
-        out_specs=(anywhere,) * 4 + (vmem,),
-        scratch_shapes=[dma((2 + 2 * parts,))],
+        in_specs=pieces + [pl.BlockSpec(router_all.shape, lambda i: (0, 0, 0))],
+        out_specs=tuple(pieces) + (pl.BlockSpec((members, experts, width), lambda i: (0, 0, 0)),),
         compiler_params=pltpu.CompilerParams(vmem_limit_bytes=60 * 1024 * 1024),
     )(*finals, router_all)
     router_grad = jnp.swapaxes(router_sum, 1, 2)

time: 323 us -> 94.2 us (0.29)
  Pallas kernels: 323 us -> 93.4 us
    pallas_call x1, Pallas kernels: 221 us -> 6.55 us  [shards(): pl.pallas_call(write_out, grid=(parts,), out_shape=tuple((jax.ShapeDtypeS...]
    pallas_call x1, Pallas kernels: 101 us -> 86.8 us  [shards(): pl.pallas_call(functools.partial(layer_kernel, (dp, members, zn, cap, tok...]
where the time goes in v4:
time: 94.2 us; the launch traced here: 94 us
  Pallas kernels  93.4 us (99%)
    pallas_call x1, Pallas kernels, shards(): pl.pallas_call(functools.partial(layer_kernel, (dp, members, zn, cap, tok...  86.8 us
    pallas_call x1, Pallas kernels, shards(): pl.pallas_call(write_out, grid=(parts,), out_shape=tuple((jax.ShapeDtypeS...  6.55 us

profile of v4, /device:TPU:0, one launch (start us, length us, event | category | flops | bytes accessed | tf_op | source)
XLA Modules:
  0.0 94.0 jit_solution(320528244331442963)
XLA Ops:
  0.6 86.8 %shard_map.101 = (bf16[2,128,1280]{2,1,0:T(8,128)(2,1)}, f32[128,1280]{1,0:T(8,128)}, bf16[1280,1152]{1,0:T(8,128)(2,1)}, bf16[1152,1280]{1,0:T(8,128)(2,1)}, f32[8,8,1280]{2,1,0:T(8,128)}) custom-call(s32[2,1,128]{2,1,0:T(1,128)} %bitcast.13, bf16[128,1280]{1,0:T(8,128)(2,1)} %tokens.1, bf16[2,128,1280]{2,1,0:T(8,128)(2,1)} %out_grad.1, ...), custom_call_target="tpu_custom_call" | custom-call | flops 6794772480 | bytes 11796480 | tf_op jit(solution)/shard_map/pallas_call | solution.py:468
  87.5 6.5 %shard_map.102 = (bf16[2,128,1280]{2,1,0:T(8,128)(2,1)}, f32[128,1280]{1,0:T(8,128)}, bf16[1280,1152]{1,0:T(8,128)(2,1)}, bf16[1152,1280]{1,0:T(8,128)(2,1)}, f32[2,4,1280]{2,1,0:T(4,128)}) custom-call(bf16[2,128,1280]{2,1,0:T(8,128)(2,1)} %get-tuple-element.15.moe, f32[128,1280]{1,0:T(8,128)} %get-tuple-element.16.grad, ...), custom_call_target="tpu_custom_call" | custom-call | tf_op jit(solution)/shard_map/pallas_call | solution.py:537

commit v5 on v4

--- a/solution.py
+++ b/solution.py
@@ -40,9 +40,9 @@
     moe_out, token_grad, first_hbm, second_hbm, router_all,
     x_send, g_send, picks, unperm, picked_router, gates, gate_grads,
     w1, w2, xr, gr, act, slope, pg, po, pd, ro, rd, first, second,
-    own, red, xch, res, router_part, router_z, router_sum,
+    own, red, xch, res, router_part, router_in, router_row, router_z, router_sum,
     load_sem, x_ss, x_rs, g_ss, g_rs, xf_ss, xf_rs, gf_ss, gf_rs, o_ss, o_rs, d_ss, d_rs,
-    red_ss, red_rs, xch_ss, xch_rs, res_ss, res_rs, rz_ss, rz_rs, rp_ss, rp_rs,
+    red_ss, red_rs, xch_ss, xch_rs, res_ss, res_rs, rz_ss, rz_rs, rp_ss, rp_rs, ri_ss, ri_rs,
 ):
     dp, members, zn, cap, toks, chunk = cfg
     peers = dp * members
@@ -62,7 +62,7 @@
         lax.fori_loop(0, count, lambda i, c: (body(i), c)[1], 0)
 
     def each_peer(body):
-        loop(peers - 1, lambda i: body((me + 1 + i) % peers))
+        loop(peers - 1, lambda i: body((me + 1 + (i + 1 - me_m) % (peers - 1)) % peers))
 
     def each_z(body):
         loop(zn - 1, lambda i: body((me_z + 1 + i) % zn))
@@ -262,14 +262,21 @@
     store1 = pltpu.make_async_copy(first, first_hbm, load_sem.at[0])
     store2 = pltpu.make_async_copy(second, second_hbm, load_sem.at[1])
 
+    def router_in_copy(to, slot):
+        return remote(
+            router_part.at[to], router_in.at[slot], ri_ss.at[to], ri_rs.at[slot], plane(to)
+        )
+
     def router_copy(z_to, z_from):
         return remote(
-            router_part, router_z.at[z_from], rz_ss.at[z_to], rz_rs.at[z_from], {"expert": z_to}
+            router_row, router_z.at[z_from], rz_ss.at[z_to], rz_rs.at[z_from], {"expert": z_to}
         )
 
     def router_plane(to, slot):
         return remote(router_sum, router_all.at[slot], rp_ss.at[to], rp_rs.at[slot], plane(to))
 
+    router_own = pltpu.make_async_copy(router_part.at[me], router_in.at[me], load_sem.at[2])
+    router_own_z = pltpu.make_async_copy(router_row, router_z.at[me_z], load_sem.at[3])
     router_mine = pltpu.make_async_copy(router_sum, router_all.at[me], load_sem.at[8])
 
     def second_grads(j):
@@ -291,15 +298,16 @@
             gate_grads[m] = partial if h == 0 else gate_grads[m] + partial
 
     def send_router():
-        total = jnp.zeros(router_part.shape, f32)
+        total = jnp.zeros((peers, width), f32)
         hot_row = lax.broadcasted_iota(jnp.int32, (members * experts, toks), 0)
         for m in range(members):
             hot = (hot_row == row_ids[m] + m * experts).astype(f32)
             weight = gate_grads[m] * gates[m] * (1.0 - gates[m])
             total += dot(hot, tokens[...].astype(f32) * weight, 1, 0, lax.Precision.HIGHEST)
-        router_part[...] = total
-        each_z(lambda z: router_copy(z, me_z).start())
-        router_z[me_z] = total
+        for p in range(peers):
+            router_part[p] = total[p : p + 1]
+        router_own.start()
+        each_peer(lambda p: router_in_copy(p, me).start())
 
     def take_dx(h):
         dxs[h][1]()
@@ -311,13 +319,24 @@
         own[base : base + dx_chunks] = total.astype(bf).reshape(dx_chunks, chunk, half)
 
     def add_router():
+        router_own.wait()
+        each_peer(lambda p: router_in_copy(p, p).wait_recv())
+        router_row[...] = jnp.sum(router_in[...], axis=0)
+        router_own_z.start()
+        each_z(lambda z: router_copy(z, me_z).start())
+
+    def share_router():
+        router_own_z.wait()
         each_z(lambda z: router_copy(z, z).wait_recv())
         router_sum[...] = jnp.sum(router_z[...], axis=0)
+        router_mine.start()
         each_peer(lambda p: router_plane(p, me).start())
-        router_mine.start()
 
     def line(source, target, send_sem, recv_sem, k, z_to):
         return remote(source.at[k], target.at[k], send_sem.at[k], recv_sem.at[k], {"expert": z_to})
+
+    loop(hidden // th, second_grads)
+    store2.start()
 
     def step(t):
         ka = t - pos
@@ -346,21 +365,20 @@
 
         @pl.when(ka == out_chunks)
         def _():
-            loop(hidden // th, second_grads)
-            store2.start()
+            loop(width // td, first_grads)
+            store1.start()
             take_out(1)
             send_router()
 
         @pl.when(ka == 2 * out_chunks)
         def _():
-            loop(width // td, first_grads)
-            store1.start()
+            take_dx(0)
             add_router()
-            take_dx(0)
 
         @pl.when(ka == 2 * out_chunks + dx_chunks)
         def _():
             take_dx(1)
+            share_router()
 
         @pl.when((ka >= 0) & (ka < chunks))
         def _():
@@ -422,13 +440,14 @@
         dxs[h][2]()
     store1.wait()
     store2.wait()
+    each_peer(lambda p: router_in_copy(p, me).wait_send())
     each_z(lambda z: router_copy(z, me_z).wait_send())
     each_peer(lambda p: router_plane(p, me).wait_send())
     each_peer(lambda p: router_plane(p, p).wait_recv())
     router_mine.wait()
 
 
-parts = 4
+parts = 8
 
 
 def write_out(moe, grad, first, second, routers, moe_to, grad_to, first_to, second_to, router_to):
@@ -439,10 +458,10 @@
 
     @pl.when(pl.program_id(0) == 0)
     def _():
-        total = jnp.sum(routers[...], axis=0)
         members, experts = router_to.shape[:2]
         for m in range(members):
-            router_to[m] = total[m * experts : (m + 1) * experts]
+            for e in range(experts):
+                router_to[m, e : e + 1] = routers[m * experts + e]
 
 
 def shards(tokens, route_ids, router, w_in, w_out, out_grad):
@@ -464,7 +483,6 @@
     block = pltpu.VMEM((peers, cap, width), bf)
     halves = pltpu.VMEM((2, peers, cap, half), bf)
     line = pltpu.VMEM((chunks, chunk, half), bf)
-    router_shape = (members * experts, width)
     moe_out, token_grad, first, second, router_all = pl.pallas_call(
         functools.partial(layer_kernel, (dp, members, zn, cap, toks, chunk)),
         out_shape=(
@@ -472,7 +490,7 @@
             jax.ShapeDtypeStruct((toks, width), f32),
             jax.ShapeDtypeStruct((width, hidden), bf),
             jax.ShapeDtypeStruct((hidden, width), bf),
-            jax.ShapeDtypeStruct((peers,) + router_shape, f32),
+            jax.ShapeDtypeStruct((peers, 1, width), f32),
         ),
         in_specs=[vmem] * 4 + [anywhere] * 2,
         out_specs=(vmem, vmem, anywhere, anywhere, anywhere),
@@ -501,16 +519,18 @@
             line,
             line,
             line,
-            pltpu.VMEM(router_shape, f32),
-            pltpu.VMEM((zn,) + router_shape, f32),
-            pltpu.VMEM(router_shape, f32),
+            pltpu.VMEM((peers, 1, width), f32),
+            pltpu.VMEM((peers, 1, width), f32),
+            pltpu.VMEM((1, width), f32),
+            pltpu.VMEM((zn, 1, width), f32),
+            pltpu.VMEM((1, width), f32),
             dma((9,)),
         ]
         + [dma((peers,))] * 8
         + [dma((2, peers))] * 4
         + [dma((chunks,))] * 6
         + [dma((zn,))] * 2
-        + [dma((peers,))] * 2,
+        + [dma((peers,))] * 4,
         compiler_params=pltpu.CompilerParams(
             collective_id=0, has_side_effects=True, vmem_limit_bytes=60 * 1024 * 1024
         ),

time: 94.2 us -> 97.9 us (1.039)
  Pallas kernels: 93.4 us -> 96.3 us
    pallas_call x1, Pallas kernels: 6.55 us -> 8.26 us  [shards(): pl.pallas_call(write_out, grid=(parts,), out_shape=tuple((jax.ShapeDtypeS...]
    pallas_call x1, Pallas kernels: 86.8 us -> 88 us  [shards(): pl.pallas_call(functools.partial(layer_kernel, (dp, members, zn, cap, tok...]
where the time goes in v5:
time: 97.9 us; the launch traced here: 96.9 us
  Pallas kernels  96.3 us (98%)
    pallas_call x1, Pallas kernels, shards(): pl.pallas_call(functools.partial(layer_kernel, (dp, members, zn, cap, tok...  88 us
    pallas_call x1, Pallas kernels, shards(): pl.pallas_call(write_out, grid=(parts,), out_shape=tuple((jax.ShapeDtypeS...  8.26 us

profile of v5, /device:TPU:0, one launch (start us, length us, event | category | flops | bytes accessed | tf_op | source)
XLA Modules:
  0.0 96.9 jit_solution(724189672388366883)
XLA Ops:
  0.6 88.0 %shard_map.101 = (bf16[2,128,1280]{2,1,0:T(8,128)(2,1)}, f32[128,1280]{1,0:T(8,128)}, bf16[1280,1152]{1,0:T(8,128)(2,1)}, bf16[1152,1280]{1,0:T(8,128)(2,1)}, f32[8,1,1280]{2,1,0:T(1,128)}) custom-call(s32[2,1,128]{2,1,0:T(1,128)} %bitcast.13, bf16[128,1280]{1,0:T(8,128)(2,1)} %tokens.1, bf16[2,128,1280]{2,1,0:T(8,128)(2,1)} %out_grad.1, ...), custom_call_target="tpu_custom_call" | custom-call | flops 6794772480 | bytes 11796480 | tf_op jit(solution)/shard_map/pallas_call | solution.py:486
  88.6 8.3 %shard_map.102 = (bf16[2,128,1280]{2,1,0:T(8,128)(2,1)}, f32[128,1280]{1,0:T(8,128)}, bf16[1280,1152]{1,0:T(8,128)(2,1)}, bf16[1152,1280]{1,0:T(8,128)(2,1)}, f32[2,4,1280]{2,1,0:T(4,128)}) custom-call(bf16[2,128,1280]{2,1,0:T(8,128)(2,1)} %get-tuple-element.15.moe, f32[128,1280]{1,0:T(8,128)} %get-tuple-element.16.grad, ...), custom_call_target="tpu_custom_call" | custom-call | tf_op jit(solution)/shard_map/pallas_call | solution.py:557

commit v6 on v5

--- a/solution.py
+++ b/solution.py
@@ -62,7 +62,7 @@
         lax.fori_loop(0, count, lambda i, c: (body(i), c)[1], 0)
 
     def each_peer(body):
-        loop(peers - 1, lambda i: body((me + 1 + (i + 1 - me_m) % (peers - 1)) % peers))
+        loop(peers - 1, lambda i: body((me + 1 + (i + (peers - 2) * me_m) % (peers - 1)) % peers))
 
     def each_z(body):
         loop(zn - 1, lambda i: body((me_z + 1 + i) % zn))
@@ -447,21 +447,40 @@
     router_mine.wait()
 
 
-parts = 8
-
-
-def write_out(moe, grad, first, second, routers, moe_to, grad_to, first_to, second_to, router_to):
-    moe_to[...] = moe[...]
-    grad_to[...] = grad[...]
-    first_to[...] = first[...]
-    second_to[...] = second[...]
-
-    @pl.when(pl.program_id(0) == 0)
-    def _():
-        members, experts = router_to.shape[:2]
-        for m in range(members):
-            for e in range(experts):
-                router_to[m, e : e + 1] = routers[m * experts + e]
+parts = 4
+
+
+def write_out(
+    first, second, moe, grad, routers, first_to, second_to, moe_to, grad_to, router_to,
+    first_held, second_held, moe_held, grad_held, in_sem, out_sem,
+):
+    trips = []
+    for source, held, target, count in (
+        (first, first_held, first_to, parts),
+        (second, second_held, second_to, parts),
+        (moe, moe_held, moe_to, 1),
+        (grad, grad_held, grad_to, 1),
+    ):
+        size = source.shape[0] // count
+        for k in range(count):
+            piece, slot = pl.ds(k * size, size), len(trips)
+            trips.append(
+                (
+                    pltpu.make_async_copy(source.at[piece], held.at[piece], in_sem.at[slot]),
+                    pltpu.make_async_copy(held.at[piece], target.at[piece], out_sem.at[slot]),
+                )
+            )
+    for fetch, _ in trips:
+        fetch.start()
+    members, experts = router_to.shape[:2]
+    for m in range(members):
+        for e in range(experts):
+            router_to[m, e : e + 1] = routers[m * experts + e]
+    for fetch, put in trips:
+        fetch.wait()
+        put.start()
+    for _, put in trips:
+        put.wait()
 
 
 def shards(tokens, route_ids, router, w_in, w_out, out_grad):
@@ -547,20 +566,15 @@
         w_in[0, 0],
         w_out[0, 0],
     )
-    finals = (moe_out, token_grad, first, second)
-    pieces = [
-        pl.BlockSpec((members, toks // parts, width), lambda i: (0, i, 0)),
-        pl.BlockSpec((toks // parts, width), lambda i: (i, 0)),
-        pl.BlockSpec((width // parts, hidden), lambda i: (i, 0)),
-        pl.BlockSpec((hidden // parts, width), lambda i: (i, 0)),
-    ]
-    moe_out, token_grad, first, second, router_sum = pl.pallas_call(
+    finals = (first, second, moe_out, token_grad)
+    first, second, moe_out, token_grad, router_sum = pl.pallas_call(
         write_out,
-        grid=(parts,),
         out_shape=tuple(jax.ShapeDtypeStruct(v.shape, v.dtype) for v in finals)
         + (jax.ShapeDtypeStruct((members, experts, width), f32),),
-        in_specs=pieces + [pl.BlockSpec(router_all.shape, lambda i: (0, 0, 0))],
-        out_specs=tuple(pieces) + (pl.BlockSpec((members, experts, width), lambda i: (0, 0, 0)),),
+        in_specs=[anywhere] * 4 + [vmem],
+        out_specs=(anywhere,) * 4 + (vmem,),
+        scratch_shapes=[pltpu.VMEM(v.shape, v.dtype) for v in finals]
+        + [dma((2 * parts + 2,))] * 2,
         compiler_params=pltpu.CompilerParams(vmem_limit_bytes=60 * 1024 * 1024),
     )(*finals, router_all)
     router_grad = jnp.swapaxes(router_sum, 1, 2)

time: 97.9 us -> 96 us (0.981)
  Pallas kernels: 96.3 us -> 94.4 us
where the time goes in v6:
time: 96 us; the launch traced here: 95.1 us
  Pallas kernels  94.4 us (98%)
    pallas_call x1, Pallas kernels, shards(): pl.pallas_call(functools.partial(layer_kernel, (dp, members, zn, cap, tok...  87.1 us
    pallas_call x1, Pallas kernels, shards(): pl.pallas_call(write_out, out_shape=tuple((jax.ShapeDtypeStruct(v.shape,...  7.29 us

profile of v6, /device:TPU:0, one launch (start us, length us, event | category | flops | bytes accessed | tf_op | source)
XLA Modules:
  0.0 95.1 jit_solution(15599551577364799427)
XLA Ops:
  0.6 87.1 %shard_map.101 = (bf16[2,128,1280]{2,1,0:T(8,128)(2,1)}, f32[128,1280]{1,0:T(8,128)}, bf16[1280,1152]{1,0:T(8,128)(2,1)}, bf16[1152,1280]{1,0:T(8,128)(2,1)}, f32[8,1,1280]{2,1,0:T(1,128)}) custom-call(s32[2,1,128]{2,1,0:T(1,128)} %bitcast.13, bf16[128,1280]{1,0:T(8,128)(2,1)} %tokens.1, bf16[2,128,1280]{2,1,0:T(8,128)(2,1)} %out_grad.1, ...), custom_call_target="tpu_custom_call" | custom-call | flops 6794772480 | bytes 11796480 | tf_op jit(solution)/shard_map/pallas_call | solution.py:505
  87.8 7.3 %shard_map.102 = (bf16[1280,1152]{1,0:T(8,128)(2,1)}, bf16[1152,1280]{1,0:T(8,128)(2,1)}, bf16[2,128,1280]{2,1,0:T(8,128)(2,1)}, f32[128,1280]{1,0:T(8,128)}, f32[2,4,1280]{2,1,0:T(4,128)}) custom-call(bf16[1280,1152]{1,0:T(8,128)(2,1)} %get-tuple-element.15.first, bf16[1152,1280]{1,0:T(8,128)(2,1)} %get-tuple-element.16.second, ...), custom_call_target="tpu_custom_call" | custom-call | tf_op jit(solution)/shard_map/pallas_call | solution.py:570
